TPU v7x, 1024 devices: a whole 4x8x16 slice. The times are simulated.
1024 devices in a mesh: sx: 16 (over y, x_hi), sy: 64 (over z, x_lo, core).
Axes of the slice: x: 4 (x_hi: 2, x_lo: 2; x = x_hi * 2 + x_lo), y: 8, z: 16, core: 2. Of those that a mesh axis runs over, the one named last changes fastest.
Arguments:
- traces: bfloat16 [16, 64, 4, 6, 16, 768], P('sx', 'sy'), may hold values from -6 to 6
- viscosity: float32 [16, 64, 4], P('sx', 'sy'), may hold values from 0.1 to 10
- partner: int32 [16, 64, 4, 4], P('sx', 'sy'), may hold values from 0 to 3, as said below
- corner_owner: int32 [16, 64, 4, 8], P('sx', 'sy'), may hold values from 0 to 511
- self_block: bfloat16 [768, 768], replicated, may hold values from -0.21875 to 0.21875
- opposite_block: bfloat16 [768, 768], replicated, may hold values from -0.21875 to 0.21875
- cross_block: bfloat16 [768, 768], replicated, may hold values from -0.21875 to 0.21875
- corner_map: bfloat16 [24, 6, 768], replicated, may hold values from -0.09375 to 0.09375
Outputs:
- applied: float32 [16, 64, 4, 6, 16, 768], P('sx', 'sy')
- coarse: float32 [48, 8192], P(None, ('sx', 'sy'))
Inputs may be any that keep to these rules, and one draw needn't show every extreme that they name: Face partners match: if the +x partner of (i, j, k) is slot p of (i+1, j), then the -x partner of (i+1, j, p) is slot k, likewise for y; each column of one device is a permutation of the 4 slots.
All inputs are finite; a program needn't handle non-finite values.
Results may differ from a plain program's by a relative error of at most 0.0042.
Values may be sent and summed in bfloat16 or wider, within the bound.
A program may use at most 32 MiB of HBM per device.

v0:
```python
import jax
import jax.numpy as jnp
from jax import lax
from jax.sharding import PartitionSpec as P

RHS = 16
CORNERS = 8
COMPS = 3
COARSE_DEV = 8


FLIP = (1, 0, 3, 2, 5, 4)


def passed_along(value, axis, steps):
    count = lax.axis_size(axis)
    first, last = (max(0, -steps), min(count, count - steps))
    return lax.ppermute(value, axis, [(source, source + steps) for source in range(first, last)])


def select_slot(received, partner_cols, column):
    slots = jnp.arange(received.shape[0], dtype=jnp.int32)
    onehot = (partner_cols[:, column][:, None] == slots[None, :]).astype(received.dtype)
    return jnp.einsum("ks,sqi->kqi", onehot, received, preferred_element_type=jnp.float32)


def facing(data, partner_cols):
    up_x = passed_along(data[:, 1], "sx", -1)
    down_x = passed_along(data[:, 0], "sx", 1)
    up_y = passed_along(data[:, 3], "sy", -1)
    down_y = passed_along(data[:, 2], "sy", 1)
    zero_sub = jnp.zeros_like(data[:1, 0]).astype(jnp.float32)
    up_z = jnp.concatenate([data[1:, 5].astype(jnp.float32), zero_sub], 0)
    down_z = jnp.concatenate([zero_sub, data[:-1, 4].astype(jnp.float32)], 0)
    faces = [
        select_slot(up_x, partner_cols, 0),
        select_slot(down_x, partner_cols, 1),
        select_slot(up_y, partner_cols, 2),
        select_slot(down_y, partner_cols, 3),
        up_z,
        down_z,
    ]
    return jnp.stack(faces, axis=1)


def body(
    traces, viscosity, partner, corner_owner, self_block, opposite_block, cross_block, corner_map
):
    values = traces[0, 0]
    partner_cols = partner[0, 0]
    flip = jnp.array(FLIP, dtype=jnp.int32)
    jumps = (values.astype(jnp.float32) - facing(values, partner_cols)).astype(jnp.bfloat16)
    shape = jumps.shape
    flat = jumps.reshape(-1, shape[-1])
    with_self = jnp.dot(flat, self_block, preferred_element_type=jnp.float32).reshape(shape)
    with_opp = jnp.dot(flat, opposite_block, preferred_element_type=jnp.float32).reshape(shape)
    with_cross = jnp.dot(flat, cross_block, preferred_element_type=jnp.float32).reshape(shape)
    adjacent = (
        jnp.sum(with_cross, axis=1, keepdims=True) - with_cross - jnp.take(with_cross, flip, axis=1)
    )
    total = with_self + jnp.take(with_opp, flip, axis=1) + adjacent
    local = (viscosity[0, 0][:, None, None, None] * total).astype(jnp.bfloat16)
    applied = local.astype(jnp.float32) - facing(local, partner_cols)
    partials = jnp.einsum("sfqi,kfi->sqk", local, corner_map, preferred_element_type=jnp.float32)
    subs = partials.shape[0]
    entries = partials.reshape(subs, RHS, CORNERS, COMPS)
    entries = jnp.transpose(entries, (0, 2, 1, 3)).reshape(subs * CORNERS, RHS * COMPS)
    owners = corner_owner[0, 0].reshape(-1)
    row_count = COARSE_DEV * lax.axis_size("sy")
    targets = jnp.arange(row_count, dtype=jnp.int32)
    onehot = (owners[:, None] == targets[None, :]).astype(jnp.float32)
    dense = jnp.dot(
        entries.T, onehot, precision=lax.Precision.HIGHEST, preferred_element_type=jnp.float32
    )
    coarse = lax.psum_scatter(dense, "sy", scatter_dimension=1, tiled=True)
    return (applied[None, None], coarse)


def solution(mesh):
    return jax.shard_map(
        body,
        mesh=mesh,
        in_specs=(
            P("sx", "sy", None, None, None, None),
            P("sx", "sy", None),
            P("sx", "sy", None, None),
            P("sx", "sy", None, None),
            P(),
            P(),
            P(),
            P(),
        ),
        out_specs=(P("sx", "sy", None, None, None, None), P(None, ("sx", "sy"))),
        check_vma=False,
    )
```

profile of v0, /device:TPU:1, one launch (start us, length us, event | category | flops | bytes accessed | tf_op | source)
XLA Modules:
  0.0 474.7 jit_solution(13118438588438596726)
XLA Ops:
  7.3 1.2 copy.125
  8.5 4.5 collective-permute-start.3
  13.0 12.8 %collective-permute-start.2 = (bf16[4,16,768]{2,1,0:T(8,128)(2,1)S(1)}, bf16[4,16,768]{2,1,0:T(8,128)(2,1)S(1)}, u32[]{:S(2)}, u32[]{:S(2)}) collective-permute-start(bf16[4,16,768]{2,1,0:T(8,128)(2,1)S(1)} %get-tuple-element.22), channel_id=1, source_target_pairs={{1,0},{2,1},{3,2},{4,3},{5,4},{6,5},{7,6},{8,7},{9,8},{10,9},{11,1... | collective-permute-start | bytes 294920 | tf_op jit(solution)/shard_map/ppermute | solution.py:18
  25.9 1.3 collective-permute-start.1
  27.2 1.3 collective-permute-start
  28.5 0.7 eq.56
  29.4 1.3 dynamic-slice
  31.4 3.7 collective-permute-done
  36.4 0.3 copy-done.1
  36.9 1.1 copy-done.2
  38.0 1.6 fusion.5
  39.6 1.3 fusion.47
  40.9 2.9 gather_fusion
  43.8 1.6 gather_fusion.1
  45.5 2.7 fusion.2
  48.9 1.3 collective-permute-start.4
  50.2 1.2 fusion.25
  51.4 1.9 collective-permute-start.7
  53.3 2.4 collective-permute-start.6
  55.7 5.5 %collective-permute-start.5 = (bf16[4,16,768]{2,1,0:T(8,128)(2,1)S(1)}, bf16[4,16,768]{2,1,0:T(8,128)(2,1)S(1)}, u32[]{:S(2)}, u32[]{:S(2)}) collective-permute-start(bf16[4,16,768]{2,1,0:T(8,128)(2,1)S(1)} %get-tuple-element.17), channel_id=1, source_target_pairs={{0,64},{64,128},{128,192},{192,256},{256,320},{320,384},{384,448},... | collective-permute-start | bytes 294920 | tf_op jit(solution)/shard_map/ppermute | solution.py:18
  61.5 2.2 collective-permute-done.5
  64.9 1.1 copy.89
  66.0 400.6 %all-reduce.7.cloned.1.call-done = f32[48,512]{0,1:T(8,128)} async-done(((f32[48,512]{0,1:T(8,128)}), f32[48,512]{0,1:T(8,128)}) %all-reduce.7.cloned.1.call-update) | async-done | bytes 98320
  466.6 1.3 constant_dynamic-slice_fusion
  (65 shorter events, 3.7 us)
Async XLA Ops:
  7.2 32.5 %copy-start = (bf16[768,768]{1,0:T(8,128)(2,1)S(1)}, bf16[768,768]{1,0:T(8,128)(2,1)}, u32[]{:S(2)}) copy-start(bf16[768,768]{1,0:T(8,128)(2,1)} %param.17) | copy-start | bytes 3538948
  7.2 24.2 %copy-start.12 = (s32[6]{0:T(128)S(1)}, s32[6]{0:T(128)}, u32[]{:S(2)}) copy-start(s32[6]{0:T(128)} %constant.48) | copy-start | bytes 76
  7.2 21.3 %copy-start.11 = (s32[1,1,4,8]{3,2,1,0:T(4,128)S(1)}, s32[1,1,4,8]{3,2,1,0:T(4,128)}, u32[]{:S(2)}) copy-start(s32[1,1,4,8]{3,2,1,0:T(4,128)} %param.14) | copy-start | bytes 388
  7.2 22.0 %copy-start.4 = (s32[1,1,4,4]{3,2,1,0:T(4,128)S(1)}, s32[1,1,4,4]{3,2,1,0:T(4,128)}, u32[]{:S(2)}) copy-start(s32[1,1,4,4]{3,2,1,0:T(4,128)} %param.13) | copy-start | bytes 196
  7.2 459.4 %all-reduce.7.cloned.1.call-start = ((), (), s32[]{:S(2)}) async-start(), calls=%async_computation | async-start | bytes 524288
  8.5 27.5 %collective-permute-start.3 = (bf16[4,16,768]{2,1,0:T(8,128)(2,1)S(1)}, bf16[4,16,768]{2,1,0:T(8,128)(2,1)S(1)}, u32[]{:S(2)}, u32[]{:S(2)}) collective-permute-start(bf16[4,16,768]{2,1,0:T(8,128)(2,1)S(1)} %get-tuple-element.21), channel_id=1, source_target_pairs={{0,1},{1,2},{2,3},{3,4},{4,5},{5,6},{6,7},{7,8},{8,9},{9,10},{10,1... | collective-permute-start | bytes 294920 | tf_op jit(solution)/shard_map/ppermute | solution.py:18
  13.0 22.7 %collective-permute-start.2 = (bf16[4,16,768]{2,1,0:T(8,128)(2,1)S(1)}, bf16[4,16,768]{2,1,0:T(8,128)(2,1)S(1)}, u32[]{:S(2)}, u32[]{:S(2)}) collective-permute-start(bf16[4,16,768]{2,1,0:T(8,128)(2,1)S(1)} %get-tuple-element.22), channel_id=1, source_target_pairs={{1,0},{2,1},{3,2},{4,3},{5,4},{6,5},{7,6},{8,7},{9,8},{10,9},{11,1... | collective-permute-start | bytes 294920 | tf_op jit(solution)/shard_map/ppermute | solution.py:18
  25.9 9.5 %collective-permute-start.1 = (bf16[4,16,768]{2,1,0:T(8,128)(2,1)S(1)}, bf16[4,16,768]{2,1,0:T(8,128)(2,1)S(1)}, u32[]{:S(2)}, u32[]{:S(2)}) collective-permute-start(bf16[4,16,768]{2,1,0:T(8,128)(2,1)S(1)} %get-tuple-element.23), channel_id=1, source_target_pairs={{0,64},{64,128},{128,192},{192,256},{256,320},{320,384},{384,448},... | collective-permute-start | bytes 294920 | tf_op jit(solution)/shard_map/ppermute | solution.py:18
  27.2 7.9 %collective-permute-start = (bf16[4,16,768]{2,1,0:T(8,128)(2,1)S(1)}, bf16[4,16,768]{2,1,0:T(8,128)(2,1)S(1)}, u32[]{:S(2)}, u32[]{:S(2)}) collective-permute-start(bf16[4,16,768]{2,1,0:T(8,128)(2,1)S(1)} %get-tuple-element.24), channel_id=1, source_target_pairs={{64,0},{128,64},{192,128},{256,192},{320,256},{384,320},{448,384},... | collective-permute-start | bytes 294920 | tf_op jit(solution)/shard_map/ppermute | solution.py:18
  29.4 6.9 %copy-start.6 = (s32[4]{0:T(128)}, s32[4]{0:T(128)S(1)}, u32[]{:S(2)}) copy-start(s32[4]{0:T(128)S(1)} %get-tuple-element.13) | copy-start | bytes 52
  29.4 6.9 %copy-start.8 = (s32[4]{0:T(128)}, s32[4]{0:T(128)S(1)}, u32[]{:S(2)}) copy-start(s32[4]{0:T(128)S(1)} %get-tuple-element.14) | copy-start | bytes 52
  35.6 1.1 copy-start.1
  36.7 1.3 copy-start.2
  43.8 1.6 copy-start.5
  45.5 2.8 copy-start.3
  48.2 2.0 copy-start.10
  48.2 13.0 %copy-start.9 = (s32[4]{0:T(128)S(1)}, s32[4]{0:T(128)}, u32[]{:S(2)}) copy-start(s32[4]{0:T(128)} %copy-done.8) | copy-start | bytes 52
  48.3 15.5 %copy-start.7 = (s32[4]{0:T(128)S(1)}, s32[4]{0:T(128)}, u32[]{:S(2)}) copy-start(s32[4]{0:T(128)} %copy-done.6) | copy-start | bytes 52
  48.9 12.4 %collective-permute-start.4 = (bf16[4,16,768]{2,1,0:T(8,128)(2,1)S(1)}, bf16[4,16,768]{2,1,0:T(8,128)(2,1)S(1)}, u32[]{:S(2)}, u32[]{:S(2)}) collective-permute-start(bf16[4,16,768]{2,1,0:T(8,128)(2,1)S(1)} %get-tuple-element.18), channel_id=1, source_target_pairs={{64,0},{128,64},{192,128},{256,192},{320,256},{384,320},{448,384},... | collective-permute-start | bytes 294920 | tf_op jit(solution)/shard_map/ppermute | solution.py:18
  51.4 13.0 %collective-permute-start.7 = (bf16[4,16,768]{2,1,0:T(8,128)(2,1)S(1)}, bf16[4,16,768]{2,1,0:T(8,128)(2,1)S(1)}, u32[]{:S(2)}, u32[]{:S(2)}) collective-permute-start(bf16[4,16,768]{2,1,0:T(8,128)(2,1)S(1)} %get-tuple-element.15), channel_id=1, source_target_pairs={{0,1},{1,2},{2,3},{3,4},{4,5},{5,6},{6,7},{7,8},{8,9},{9,10},{10,1... | collective-permute-start | bytes 294920 | tf_op jit(solution)/shard_map/ppermute | solution.py:18
  53.3 10.7 %collective-permute-start.6 = (bf16[4,16,768]{2,1,0:T(8,128)(2,1)S(1)}, bf16[4,16,768]{2,1,0:T(8,128)(2,1)S(1)}, u32[]{:S(2)}, u32[]{:S(2)}) collective-permute-start(bf16[4,16,768]{2,1,0:T(8,128)(2,1)S(1)} %get-tuple-element.16), channel_id=1, source_target_pairs={{1,0},{2,1},{3,2},{4,3},{5,4},{6,5},{7,6},{8,7},{9,8},{10,9},{11,1... | collective-permute-start | bytes 294920 | tf_op jit(solution)/shard_map/ppermute | solution.py:18
  55.7 8.0 %collective-permute-start.5 = (bf16[4,16,768]{2,1,0:T(8,128)(2,1)S(1)}, bf16[4,16,768]{2,1,0:T(8,128)(2,1)S(1)}, u32[]{:S(2)}, u32[]{:S(2)}) collective-permute-start(bf16[4,16,768]{2,1,0:T(8,128)(2,1)S(1)} %get-tuple-element.17), channel_id=1, source_target_pairs={{0,64},{64,128},{128,192},{192,256},{256,320},{320,384},{384,448},... | collective-permute-start | bytes 294920 | tf_op jit(solution)/shard_map/ppermute | solution.py:18
Sparse Core Ops, SparseCore 0:
  51.5 415.0 all-reduce.6
where the time goes:
time: 475 us
  waiting for transfers between devices  407 us (86%)
  starting transfers between devices  31.1 us (7%)
  between operations  15.2 us (3%)
  local copies, waits for them, and re-layouts  12.4 us (3%)
  matrix products  9.08 us (2%)
    unnamed x2, waiting for transfers between devices  401 us
    ppermute x8, starting transfers between devices, passed_along(): lax.ppermute(value, axis, [(source, source + steps) for source in range(f...  31.1 us
  transfers between devices with their start and end apart: 9, of which 3 were waited for; matrix products, arithmetic and copies ran while one was open for 1% of the time, Pallas kernels for 0%

commit v1 on v0

v1 whole, which is shorter than its diff:
```python
import functools

import jax
import jax.numpy as jnp
from jax import lax
from jax.experimental import pallas as pl
from jax.experimental.pallas import tpu as pltpu
from jax.sharding import PartitionSpec as P

MESH = pl.DeviceIdType.MESH
F32, BF16 = jnp.float32, jnp.bfloat16
SUBS = 4
RHS = 16
HALF = 8
CORNERS = 8
COMPS = 3
KEYS = CORNERS * COMPS
BLOCK = 32
QUAD = 4
OPP = (1, 0, 3, 2, 5, 4)


def nt_dot(left, right):
    return lax.dot_general(left, right, (((1,), (1,)), ((), ())), preferred_element_type=F32)


def split(value, parts):
    out = []
    for _ in range(parts):
        head = value.astype(BF16)
        out.append(head)
        value = value - head.astype(F32)
    return out


def kernel(
    nx, ny,
    traces, visc_in, partner_in, owner_in, self_in, opp_in, cross_in, cmap_in,
    applied, coarse,
    raw, s_mat, o_mat, c_mat, cmap, visc, partner, owner,
    own, out1, in1, jump, w_s, w_o, w_c, local, in2,
    w_hi, w_lo, y_all, y_out, y_in, dense, z_in, quad_out, quad_in,
    load_sem, send1, recv1, send2, recv2, send_y, recv_y, send_z, recv_z, send_q, recv_q, far_sem,
):
    width = raw.shape[-1]
    nz = ny // QUAD
    reach = nz // 4
    sx, sy = lax.axis_index("sx"), lax.axis_index("sy")
    z, quad = sy // QUAD, lax.rem(sy, QUAD)

    def in_row(to):
        return (sx, lax.rem(to + ny, ny))

    beside = (
        (lax.rem(sx + 1, nx), sy),
        (lax.rem(sx + nx - 1, nx), sy),
        in_row(sy + 1),
        in_row(sy - 1),
    )
    inside = (sx < nx - 1, sx > 0, sy < ny - 1, sy > 0)
    quads = [(sx, z * QUAD + lax.rem(quad + j, QUAD)) for j in range(1, QUAD)]
    near = [in_row(sy + QUAD * d) for d in range(1, reach + 1)]
    near += [in_row(sy - QUAD * d) for d in range(1, reach + 1)]

    barrier = pltpu.get_barrier_semaphore()
    greeted = [*beside, *quads, *near]
    for device in greeted:
        pl.semaphore_signal(barrier, inc=1, device_id=device, device_id_type=MESH)

    loads = {}
    for i, (name, source, target) in enumerate((
        ("raw", traces.at[0, 0], raw),
        ("cmap", cmap_in, cmap),
        ("cross", cross_in, c_mat),
        ("self", self_in, s_mat),
        ("opp", opp_in, o_mat),
        ("visc", visc_in.at[0, 0], visc),
        ("partner", partner_in.at[0, 0], partner),
        ("owner", owner_in.at[0, 0], owner),
    )):
        loads[name] = pltpu.make_async_copy(source, target, load_sem.at[i])
        loads[name].start()

    def exchange(source, target, sends, recvs, f):
        copy = pltpu.make_async_remote_copy(
            src_ref=source,
            dst_ref=target.at[OPP[f]],
            send_sem=sends.at[f],
            recv_sem=recvs.at[OPP[f]],
            device_id=beside[f],
            device_id_type=MESH,
        )
        copy.start()
        return copy

    with jax.named_scope("repack"):
        loads["raw"].wait()
        for f in range(6):
            for s in range(SUBS):
                both = raw[s, f].astype(F32)
                for c in range(2):
                    own[c, f, s] = both[c * HALF : (c + 1) * HALF]
            if f < 4:
                for c in range(2):
                    out1[c, f] = own[c, f].reshape(SUBS * HALF, width).astype(BF16)

    with jax.named_scope("entry"):
        pl.semaphore_wait(barrier, len(greeted))

    copies1 = [[exchange(out1.at[0, f], in1.at[0], send1.at[0], recv1.at[0], f) for f in range(4)]]
    for device in (in_row(sy + QUAD * reach), in_row(sy - QUAD * reach)):
        pl.semaphore_signal(far_sem, inc=1, device_id=device, device_id_type=MESH)

    lane = lax.broadcasted_iota(jnp.int32, (1, 128), 1)
    block = lane // BLOCK

    def moved(value, shift):
        shift = (shift * BLOCK) % 128
        return pltpu.roll(value, shift, 1) if shift else value

    with jax.named_scope("weights"):
        loads["cmap"].wait()
        pad = jnp.zeros((BLOCK - KEYS, width), F32)
        faces = [jnp.concatenate([cmap[f].astype(F32), pad], 0) for f in range(6)]
        pairs = [faces[0] + faces[1], faces[2] + faces[3], faces[4] + faces[5]]
        adjacent = [pairs[1] + pairs[2], pairs[0] + pairs[2], pairs[0] + pairs[1]]
        adjacent = jnp.concatenate([adjacent[f // 2] for f in range(6)], 0)
        adj_hi, adj_lo = split(adjacent, 2)
        straight = jnp.concatenate(faces, 0).astype(BF16)
        flipped = jnp.concatenate([faces[OPP[f]] for f in range(6)], 0).astype(BF16)
        loads["cross"].wait()
        weight = nt_dot(adj_hi, c_mat[...]) + nt_dot(adj_lo, c_mat[...])
        loads["self"].wait()
        weight += nt_dot(straight, s_mat[...])
        loads["opp"].wait()
        weight += nt_dot(flipped, o_mat[...])
        w_hi[...], w_lo[...] = split(weight, 2)

    with jax.named_scope("corner_values"):
        flat = raw[...].reshape(SUBS * 6 * RHS, width)
        both = nt_dot(flat, w_hi[...]) + nt_dot(flat, w_lo[...])
        y_all[...] = both.reshape(SUBS, 6, RHS, 6 * BLOCK)

        def value_of(s, f, face, to):
            if face < 4:
                tile, at = y_all[s, f, :, :128], face
            else:
                tile = y_all[s, f, :, 128:]
                tile = jnp.concatenate([tile, jnp.zeros((RHS, 64), F32)], 1)
                at = face - 4
            return jnp.where(block == to, moved(tile, to - at), 0.0)

        copies_y = []
        for f in range(4):
            y_out[f] = sum(value_of(s, f, OPP[f], s) for s in range(SUBS))
            copies_y.append(exchange(y_out.at[f], y_in, send_y, recv_y, f))

    copies1.append([exchange(out1.at[1, f], in1.at[1], send1.at[1], recv1.at[1], f) for f in range(4)])

    with jax.named_scope("own_corners"):
        for name in ("visc", "partner", "owner"):
            loads[name].wait()
        parts = jnp.zeros((RHS, 128), F32)
        for s in range(SUBS):
            for f in range(6):
                parts += value_of(s, f, f, s)
            if s < SUBS - 1:
                parts -= value_of(s + 1, 5, 4, s)
            if s > 0:
                parts -= value_of(s - 1, 4, 5, s)
        visc_lanes = jnp.zeros((1, 128), F32)
        for s in range(SUBS):
            visc_lanes = jnp.where(block == s, visc[s], visc_lanes)
        row = lax.broadcasted_iota(jnp.int32, (SUBS * BLOCK, 1), 0)
        owners = jnp.full((SUBS * BLOCK, 1), -1, jnp.int32)
        for s in range(SUBS):
            for m in range(CORNERS):
                first = s * BLOCK + m * COMPS
                owners = jnp.where((row >= first) & (row < first + COMPS), owner[s, m], owners)
        unknown = lax.broadcasted_iota(jnp.int32, (SUBS * BLOCK, 8 * ny), 1)
        onehot = jnp.where(unknown == owners, 1.0, 0.0).astype(BF16)

    with jax.named_scope("corners"):
        for f in range(4):
            copies_y[f].wait_recv()
        for f in range(4):
            received = y_in[f]
            slots = jnp.zeros((1, 128), jnp.int32)
            for s in range(SUBS):
                slots = jnp.where(block == s, partner[s, f], slots)
            chosen = jnp.zeros((RHS, 128), F32)
            for d in range(SUBS):
                here = slots == lax.rem(block - d + SUBS, SUBS)
                chosen += jnp.where(here, moved(received, d), 0.0)
            parts -= jnp.where(inside[f], chosen, 0.0)
        parts = parts * visc_lanes
        comp = lax.rem(lax.rem(lane, BLOCK), COMPS)
        stacked = jnp.concatenate([jnp.where(comp == c, parts, 0.0) for c in range(COMPS)], 0)
        rows = COMPS * RHS
        total = jnp.dot(
            jnp.concatenate(split(stacked, 3), 0), onehot, preferred_element_type=F32
        )
        total = total[:rows] + total[rows : 2 * rows] + total[2 * rows :]
        for to in range(nz):
            tiles = total[:, to // 4 * 128 : to // 4 * 128 + 128]
            halves = []
            for groups in ((0, 1, 2, 3), (4, 5)):
                half = jnp.zeros((8, 128), F32)
                for g in groups:
                    value = moved(tiles[g * 8 : g * 8 + 8], g % 4 - to % 4)
                    half = jnp.where(block == g % 4, value, half)
                halves.append(half)
            dense[to] = jnp.concatenate(halves, 0)

    with jax.named_scope("corner_send"):
        pl.semaphore_wait(far_sem, 2)
        order = sorted(range(1, nz), key=lambda d: -min(d, nz - d))
        copies_z = {}
        for d in order:
            copies_z[d] = pltpu.make_async_remote_copy(
                src_ref=dense.at[lax.rem(z + d, nz)],
                dst_ref=z_in.at[d],
                send_sem=send_z.at[d],
                recv_sem=recv_z.at[d],
                device_id=in_row(sy + QUAD * d),
                device_id_type=MESH,
            )
            copies_z[d].start()

    def selected(f, received):
        received = received.astype(F32)
        slots = [received[p * HALF : (p + 1) * HALF] for p in range(SUBS)]
        values = []
        for s in range(SUBS):
            value = slots[0]
            for p in range(1, SUBS):
                value = jnp.where(partner[s, f] == p, slots[p], value)
            values.append(value)
        values = jnp.concatenate(values, 0)
        return jnp.where(inside[f], values, 0.0)

    none = jnp.zeros((HALF, width), F32)
    visc_rows = jnp.concatenate([jnp.full((HALF, width), visc[s], F32) for s in range(SUBS)], 0)
    size = SUBS * HALF

    copies2 = []
    for c in range(2):
        with jax.named_scope(f"wait_traces{c}"):
            for f in range(4):
                copies1[c][f].wait_recv()
        with jax.named_scope(f"local{c}"):
            for f in range(4):
                mine = own[c, f].reshape(size, width)
                jump[f * size : (f + 1) * size] = (mine - selected(f, in1[c, f])).astype(BF16)
            top, bottom = own[c, 4].reshape(size, width), own[c, 5].reshape(size, width)
            above = jnp.concatenate([bottom[HALF:], none], 0)
            below = jnp.concatenate([none, top[:-HALF]], 0)
            jump[4 * size : 5 * size] = (top - above).astype(BF16)
            jump[5 * size : 6 * size] = (bottom - below).astype(BF16)
            w_c[...] = jnp.dot(jump[...], c_mat[...], preferred_element_type=F32)
            w_s[...] = jnp.dot(jump[...], s_mat[...], preferred_element_type=F32)
            w_o[...] = jnp.dot(jump[...], o_mat[...], preferred_element_type=F32)

            def face(ref, f):
                return ref[f * size : (f + 1) * size]

            copies2.append([])
            for f in range(6):
                others = [g for g in range(6) if g // 2 != f // 2]
                value = face(w_s, f) + face(w_o, OPP[f])
                value += (face(w_c, others[0]) + face(w_c, others[1])) + (
                    face(w_c, others[2]) + face(w_c, others[3])
                )
                local[c, f] = (visc_rows * value).astype(BF16)
                if f < 4:
                    copies2[c].append(exchange(local.at[c, f], in2.at[c], send2.at[c], recv2.at[c], f))
            top, bottom = local[c, 4].astype(F32), local[c, 5].astype(F32)
            above = jnp.concatenate([bottom[HALF:], none], 0)
            below = jnp.concatenate([none, top[:-HALF]], 0)
            for f, value in ((4, top - above), (5, bottom - below)):
                for s in range(SUBS):
                    applied[0, 0, s, f, c * HALF : (c + 1) * HALF] = value[s * HALF : (s + 1) * HALF]

    def finish(c):
        with jax.named_scope(f"wait_local{c}"):
            for f in range(4):
                copies2[c][f].wait_recv()
        with jax.named_scope(f"applied{c}"):
            for f in range(4):
                value = local[c, f].astype(F32) - selected(f, in2[c, f])
                for s in range(SUBS):
                    applied[0, 0, s, f, c * HALF : (c + 1) * HALF] = value[s * HALF : (s + 1) * HALF]

    with jax.named_scope("corner_sum"):
        for d in range(1, nz):
            copies_z[d].wait_recv()
        values = [dense[z]] + [z_in[d] for d in range(1, nz)]
        while len(values) > 1:
            values = [a + b for a, b in zip(values[::2], values[1::2])] + values[len(values) & ~1 :]
        quad_out[...] = values[0]
        copies_q = []
        for j in range(1, QUAD):
            copies_q.append(pltpu.make_async_remote_copy(
                src_ref=quad_out,
                dst_ref=quad_in.at[j],
                send_sem=send_q.at[j],
                recv_sem=recv_q.at[j],
                device_id=quads[j - 1],
                device_id_type=MESH,
            ))
            copies_q[-1].start()

    finish(0)

    with jax.named_scope("corner_end"):
        for copy in copies_q:
            copy.wait_recv()
        result = (quad_out[...] + quad_in[1]) + (quad_in[2] + quad_in[3])
        mine = result
        for j in range(1, QUAD):
            mine = jnp.where(quad == j, pltpu.roll(result, 128 - 8 * j, 1), mine)
        for g in range(6):
            value = moved(mine[g // 4 * 8 : g // 4 * 8 + 8], -(g % 4))
            coarse[pl.ds(g % 2 * HALF * COMPS + g // 2, HALF, stride=COMPS)] = value

    finish(1)

    with jax.named_scope("sent"):
        for copy in [*copies1[0], *copies1[1], *copies_y, *copies_z.values(), *copies_q, *copies2[0], *copies2[1]]:
            copy.wait_send()


def body(traces, viscosity, partner, corner_owner, self_block, opposite_block, cross_block, corner_map):
    nx, ny = lax.axis_size("sx"), lax.axis_size("sy")
    width = traces.shape[-1]
    nz = ny // QUAD
    vmem, dma = pltpu.VMEM, pltpu.SemaphoreType.DMA
    size = SUBS * HALF
    applied, coarse = pl.pallas_call(
        functools.partial(kernel, nx, ny),
        out_shape=(
            jax.ShapeDtypeStruct(traces.shape, F32),
            jax.ShapeDtypeStruct((RHS * COMPS, 128), F32),
        ),
        in_specs=[pl.BlockSpec(memory_space=pltpu.HBM)] * 8,
        out_specs=(pl.BlockSpec(memory_space=vmem), pl.BlockSpec(memory_space=vmem)),
        scratch_shapes=[
            vmem((SUBS, 6, RHS, width), BF16),
            vmem((width, width), BF16),
            vmem((width, width), BF16),
            vmem((width, width), BF16),
            vmem((6, KEYS, width), BF16),
            pltpu.SMEM((SUBS,), F32),
            pltpu.SMEM((SUBS, 4), jnp.int32),
            pltpu.SMEM((SUBS, CORNERS), jnp.int32),
            vmem((2, 6, SUBS, HALF, width), F32),
            vmem((2, 4, size, width), BF16),
            vmem((2, 4, size, width), BF16),
            vmem((6 * size, width), BF16),
            vmem((6 * size, width), F32),
            vmem((6 * size, width), F32),
            vmem((6 * size, width), F32),
            vmem((2, 6, size, width), BF16),
            vmem((2, 4, size, width), BF16),
            vmem((6 * BLOCK, width), BF16),
            vmem((6 * BLOCK, width), BF16),
            vmem((SUBS, 6, RHS, 6 * BLOCK), F32),
            vmem((4, RHS, 128), F32),
            vmem((4, RHS, 128), F32),
            vmem((nz, 16, 128), F32),
            vmem((nz, 16, 128), F32),
            vmem((16, 128), F32),
            vmem((QUAD, 16, 128), F32),
            dma((8,)),
            dma((2, 4)),
            dma((2, 4)),
            dma((2, 4)),
            dma((2, 4)),
            dma((4,)),
            dma((4,)),
            dma((nz,)),
            dma((nz,)),
            dma((QUAD,)),
            dma((QUAD,)),
            pltpu.SemaphoreType.REGULAR,
        ],
        compiler_params=pltpu.CompilerParams(
            collective_id=0, has_side_effects=True, vmem_limit_bytes=40 * 2**20
        ),
    )(traces, viscosity, partner, corner_owner, self_block, opposite_block, cross_block, jnp.transpose(corner_map, (1, 0, 2)))
    return applied, coarse[:, :8]


def solution(mesh):
    return jax.shard_map(
        body,
        mesh=mesh,
        in_specs=(
            P("sx", "sy", None, None, None, None),
            P("sx", "sy", None),
            P("sx", "sy", None, None),
            P("sx", "sy", None, None),
            P(),
            P(),
            P(),
            P(),
        ),
        out_specs=(P("sx", "sy", None, None, None, None), P(None, ("sx", "sy"))),
        check_vma=False,
    )
```

time: 475 us -> 51.7 us (0.11)
  waiting for transfers between devices: 407 us -> 0 us
  Pallas kernels: 0 us -> 41 us
  starting transfers between devices: 31.1 us -> 0 us
  between operations: 15.2 us -> 0.66 us
  matrix products: 9.08 us -> 0 us
    unnamed x2 -> x0, waiting for transfers between devices: 401 us -> none
    pallas_call x0 -> x1, Pallas kernels: none -> 41 us  [body(): pl.pallas_call(functools.partial(kernel, nx, ny), out_shape=(jax.ShapeDty...]
    ppermute x8 -> x0, starting transfers between devices: 31.1 us -> none  [passed_along(): lax.ppermute(value, axis, [(source, source + steps) for source in range(f...]
    dot_general x13 -> x0, matrix products: 9.08 us -> none  [the longest x1 2.67 us: body(): jnp.dot(flat, self_block, preferred_element_type=jnp.float32).reshape(shape)]
    ppermute x8 -> x0, waiting for transfers between devices: 5.9 us -> none  [passed_along(): lax.ppermute(value, axis, [(source, source + steps) for source in range(f...]
  transfers between devices with their start and end apart: 9 -> 0, of which waited for: 3 -> 0; matrix products, arithmetic and copies ran while one was open for 1% -> 0% of each run, Pallas kernels for 0% -> 0%
where the time goes in v1:
time: 51.7 us; the launch traced here: 51.2 us
  Pallas kernels  41 us (79%)
  local copies, waits for them, and re-layouts  9.49 us (18%)
  between operations  0.66 us (1%)
    pallas_call x1, Pallas kernels, body(): pl.pallas_call(functools.partial(kernel, nx, ny), out_shape=(jax.ShapeDty...  41 us
    unnamed x18, local copies, waits for them, and re-layouts  9.49 us

profile of v1, /device:TPU:1, one launch (start us, length us, event | category | flops | bytes accessed | tf_op | source)
XLA Modules:
  0.0 51.2 jit_solution(12633055965291235414)
XLA Ops:
  0.6 0.0 copy-start
  0.6 1.3 %copy-done = bf16[768,768]{1,0:T(8,128)(2,1)S(1)} copy-done((bf16[768,768]{1,0:T(8,128)(2,1)S(1)}, bf16[768,768]{1,0:T(8,128)(2,1)}, u32[]{:S(2)}) %copy-start) | copy-done | bytes 1179672
  1.9 0.0 copy-start.1
  1.9 1.3 %copy-done.1 = bf16[768,768]{1,0:T(8,128)(2,1)S(1)} copy-done((bf16[768,768]{1,0:T(8,128)(2,1)S(1)}, bf16[768,768]{1,0:T(8,128)(2,1)}, u32[]{:S(2)}) %copy-start.1) | copy-done | bytes 1179672
  3.2 0.0 copy-start.2
  3.2 1.3 %copy-done.2 = bf16[768,768]{1,0:T(8,128)(2,1)S(1)} copy-done((bf16[768,768]{1,0:T(8,128)(2,1)S(1)}, bf16[768,768]{1,0:T(8,128)(2,1)}, u32[]{:S(2)}) %copy-start.2) | copy-done | bytes 1179672
  4.4 0.0 copy-start.3
  4.4 1.1 %copy-done.3 = bf16[1,1,4,6,16,768]{5,4,3,2,1,0:T(8,128)(2,1)S(1)} copy-done((bf16[1,1,4,6,16,768]{5,4,3,2,1,0:T(8,128)(2,1)S(1)}, bf16[1,1,4,6,16,768]{5,4,3,2,1,0:T(8,128)(2,1)}, u32[]{:S(2)}) %copy-start.3) | copy-done | bytes 589848
  5.5 0.0 copy-start.4
  5.5 0.9 %copy-done.4 = bf16[24,6,768]{2,0,1:T(8,128)(2,1)S(1)} copy-done((bf16[24,6,768]{2,0,1:T(8,128)(2,1)S(1)}, bf16[24,6,768]{2,0,1:T(8,128)(2,1)}, u32[]{:S(2)}) %copy-start.4) | copy-done | bytes 221208
  6.4 0.0 copy-start.5
  6.4 0.7 %copy-done.5 = s32[1,1,4,4]{3,2,1,0:T(4,128)S(1)} copy-done((s32[1,1,4,4]{3,2,1,0:T(4,128)S(1)}, s32[1,1,4,4]{3,2,1,0:T(4,128)}, u32[]{:S(2)}) %copy-start.5) | copy-done | bytes 88
  7.1 0.0 copy-start.6
  7.1 0.7 %copy-done.6 = s32[1,1,4,8]{3,2,1,0:T(4,128)S(1)} copy-done((s32[1,1,4,8]{3,2,1,0:T(4,128)S(1)}, s32[1,1,4,8]{3,2,1,0:T(4,128)}, u32[]{:S(2)}) %copy-start.6) | copy-done | bytes 152
  7.8 0.0 copy-start.7
  7.8 0.7 %copy-done.7 = f32[1,1,4]{2,1,0:T(1,128)S(1)} copy-done((f32[1,1,4]{2,1,0:T(1,128)S(1)}, f32[1,1,4]{2,1,0:T(1,128)}, u32[]{:S(2)}) %copy-start.7) | copy-done | bytes 40
  8.5 41.0 %shard_map.95 = (f32[1,1,4,6,16,768]{5,4,3,2,1,0:T(8,128)S(1)}, f32[48,128]{1,0:T(8,128)S(1)}) custom-call(bf16[1,1,4,6,16,768]{5,4,3,2,1,0:T(8,128)(2,1)S(1)} %copy-done.3, f32[1,1,4]{2,1,0:T(1,128)S(1)} %copy-done.7, s32[1,1,4,4]{3,2,1,0:T(4,128)S(1)} %copy-done.5, s32[1,1,4,8]{3,2,1,0:T(4,128)S(1)} %copy-done.6, bf16[768,768]{1,0:T(8,128)(2,1)S(1)} %copy-done, ...), custom_call_target="tpu_custom_call" | custom-call | tf_op jit(solution)/shard_map/pallas_call | solution.py:339
  49.5 0.7 %copy.10 = f32[48,8]{0,1:T(8,128)} copy(f32[48,8]{1,0:T(8,128)S(1)} %bitcast.3) | data formatting | bytes 3072
  50.2 1.0 %copy.12 = f32[1,1,4,6,16,768]{5,4,3,2,1,0:T(8,128)} copy(f32[1,1,4,6,16,768]{5,4,3,2,1,0:T(8,128)S(1)} %get-tuple-element.10) | data formatting | bytes 2359296
Async XLA Ops:
  0.6 1.3 %copy-start = (bf16[768,768]{1,0:T(8,128)(2,1)S(1)}, bf16[768,768]{1,0:T(8,128)(2,1)}, u32[]{:S(2)}) copy-start(bf16[768,768]{1,0:T(8,128)(2,1)} %self_in.1) | copy-start | bytes 3538948
  1.9 1.3 %copy-start.1 = (bf16[768,768]{1,0:T(8,128)(2,1)S(1)}, bf16[768,768]{1,0:T(8,128)(2,1)}, u32[]{:S(2)}) copy-start(bf16[768,768]{1,0:T(8,128)(2,1)} %opp_in.1) | copy-start | bytes 3538948
  3.2 1.3 %copy-start.2 = (bf16[768,768]{1,0:T(8,128)(2,1)S(1)}, bf16[768,768]{1,0:T(8,128)(2,1)}, u32[]{:S(2)}) copy-start(bf16[768,768]{1,0:T(8,128)(2,1)} %cross_in.1) | copy-start | bytes 3538948
  4.4 1.1 %copy-start.3 = (bf16[1,1,4,6,16,768]{5,4,3,2,1,0:T(8,128)(2,1)S(1)}, bf16[1,1,4,6,16,768]{5,4,3,2,1,0:T(8,128)(2,1)}, u32[]{:S(2)}) copy-start(bf16[1,1,4,6,16,768]{5,4,3,2,1,0:T(8,128)(2,1)} %traces.1) | copy-start | bytes 1769476
  5.5 0.9 %copy-start.4 = (bf16[24,6,768]{2,0,1:T(8,128)(2,1)S(1)}, bf16[24,6,768]{2,0,1:T(8,128)(2,1)}, u32[]{:S(2)}) copy-start(bf16[24,6,768]{2,0,1:T(8,128)(2,1)} %param.15) | copy-start | bytes 663556
  6.4 0.7 %copy-start.5 = (s32[1,1,4,4]{3,2,1,0:T(4,128)S(1)}, s32[1,1,4,4]{3,2,1,0:T(4,128)}, u32[]{:S(2)}) copy-start(s32[1,1,4,4]{3,2,1,0:T(4,128)} %partner_in.1) | copy-start | bytes 196
  7.1 0.7 %copy-start.6 = (s32[1,1,4,8]{3,2,1,0:T(4,128)S(1)}, s32[1,1,4,8]{3,2,1,0:T(4,128)}, u32[]{:S(2)}) copy-start(s32[1,1,4,8]{3,2,1,0:T(4,128)} %owner_in.1) | copy-start | bytes 388
  7.8 0.7 %copy-start.7 = (f32[1,1,4]{2,1,0:T(1,128)S(1)}, f32[1,1,4]{2,1,0:T(1,128)}, u32[]{:S(2)}) copy-start(f32[1,1,4]{2,1,0:T(1,128)} %visc_in.1) | copy-start | bytes 52

commit v2 on v1

--- a/solution.py
+++ b/solution.py
@@ -39,8 +39,8 @@
     applied, coarse,
     raw, s_mat, o_mat, c_mat, cmap, visc, partner, owner,
     own, out1, in1, jump, w_s, w_o, w_c, local, in2,
-    w_hi, w_lo, y_all, y_out, y_in, dense, z_in, quad_out, quad_in,
-    load_sem, send1, recv1, send2, recv2, send_y, recv_y, send_z, recv_z, send_q, recv_q, far_sem,
+    w_hi, w_lo, dense, z_in, quad_out, quad_in,
+    load_sem, send1, recv1, send2, recv2, send_z, recv_z, send_q, recv_q, far_sem,
 ):
     width = raw.shape[-1]
     nz = ny // QUAD
@@ -64,8 +64,9 @@
 
     barrier = pltpu.get_barrier_semaphore()
     greeted = [*beside, *quads, *near]
-    for device in greeted:
-        pl.semaphore_signal(barrier, inc=1, device_id=device, device_id_type=MESH)
+    with jax.named_scope("greet"):
+        for device in greeted:
+            pl.semaphore_signal(barrier, inc=1, device_id=device, device_id_type=MESH)
 
     loads = {}
     for i, (name, source, target) in enumerate((
@@ -107,7 +108,10 @@
     with jax.named_scope("entry"):
         pl.semaphore_wait(barrier, len(greeted))
 
-    copies1 = [[exchange(out1.at[0, f], in1.at[0], send1.at[0], recv1.at[0], f) for f in range(4)]]
+    copies1 = [
+        [exchange(out1.at[c, f], in1.at[c], send1.at[c], recv1.at[c], f) for f in range(4)]
+        for c in range(2)
+    ]
     for device in (in_row(sy + QUAD * reach), in_row(sy - QUAD * reach)):
         pl.semaphore_signal(far_sem, inc=1, device_id=device, device_id_type=MESH)
 
@@ -134,40 +138,12 @@
         weight += nt_dot(straight, s_mat[...])
         loads["opp"].wait()
         weight += nt_dot(flipped, o_mat[...])
-        w_hi[...], w_lo[...] = split(weight, 2)
-
-    with jax.named_scope("corner_values"):
-        flat = raw[...].reshape(SUBS * 6 * RHS, width)
-        both = nt_dot(flat, w_hi[...]) + nt_dot(flat, w_lo[...])
-        y_all[...] = both.reshape(SUBS, 6, RHS, 6 * BLOCK)
-
-        def value_of(s, f, face, to):
-            if face < 4:
-                tile, at = y_all[s, f, :, :128], face
-            else:
-                tile = y_all[s, f, :, 128:]
-                tile = jnp.concatenate([tile, jnp.zeros((RHS, 64), F32)], 1)
-                at = face - 4
-            return jnp.where(block == to, moved(tile, to - at), 0.0)
-
-        copies_y = []
-        for f in range(4):
-            y_out[f] = sum(value_of(s, f, OPP[f], s) for s in range(SUBS))
-            copies_y.append(exchange(y_out.at[f], y_in, send_y, recv_y, f))
-
-    copies1.append([exchange(out1.at[1, f], in1.at[1], send1.at[1], recv1.at[1], f) for f in range(4)])
-
-    with jax.named_scope("own_corners"):
+        rest = jnp.zeros((2 * BLOCK, width), F32)
+        w_hi[...], w_lo[...] = split(jnp.concatenate([weight, rest], 0), 2)
+
+    with jax.named_scope("owners"):
         for name in ("visc", "partner", "owner"):
             loads[name].wait()
-        parts = jnp.zeros((RHS, 128), F32)
-        for s in range(SUBS):
-            for f in range(6):
-                parts += value_of(s, f, f, s)
-            if s < SUBS - 1:
-                parts -= value_of(s + 1, 5, 4, s)
-            if s > 0:
-                parts -= value_of(s - 1, 4, 5, s)
         visc_lanes = jnp.zeros((1, 128), F32)
         for s in range(SUBS):
             visc_lanes = jnp.where(block == s, visc[s], visc_lanes)
@@ -180,20 +156,33 @@
         unknown = lax.broadcasted_iota(jnp.int32, (SUBS * BLOCK, 8 * ny), 1)
         onehot = jnp.where(unknown == owners, 1.0, 0.0).astype(BF16)
 
-    with jax.named_scope("corners"):
-        for f in range(4):
-            copies_y[f].wait_recv()
-        for f in range(4):
-            received = y_in[f]
-            slots = jnp.zeros((1, 128), jnp.int32)
-            for s in range(SUBS):
-                slots = jnp.where(block == s, partner[s, f], slots)
-            chosen = jnp.zeros((RHS, 128), F32)
-            for d in range(SUBS):
-                here = slots == lax.rem(block - d + SUBS, SUBS)
-                chosen += jnp.where(here, moved(received, d), 0.0)
-            parts -= jnp.where(inside[f], chosen, 0.0)
-        parts = parts * visc_lanes
+    def selected(f, received):
+        received = received.astype(F32)
+        slots = [received[p * HALF : (p + 1) * HALF] for p in range(SUBS)]
+        values = []
+        for s in range(SUBS):
+            value = slots[0]
+            for p in range(1, SUBS):
+                value = jnp.where(partner[s, f] == p, slots[p], value)
+            values.append(value)
+        values = jnp.concatenate(values, 0)
+        return jnp.where(inside[f], values, 0.0)
+
+    none = jnp.zeros((HALF, width), F32)
+    visc_rows = jnp.concatenate([jnp.full((HALF, width), visc[s], F32) for s in range(SUBS)], 0)
+    size = SUBS * HALF
+
+    def corner_values(pairs):
+        values = jnp.zeros((HALF, 128), F32)
+        for s in range(SUBS):
+            rows = [pairs[f * size + s * HALF : f * size + (s + 1) * HALF] for f in range(6)]
+            tiles = [rows[f][:, f // 4 * 128 : f // 4 * 128 + 128] for f in range(6)]
+            tiles = [tiles[0] + tiles[4], tiles[1] + tiles[5], tiles[2], tiles[3]]
+            for f in range(4):
+                values += jnp.where(block == s, moved(tiles[f], s - f), 0.0)
+        return values * visc_lanes
+
+    def send_corners(parts):
         comp = lax.rem(lax.rem(lane, BLOCK), COMPS)
         stacked = jnp.concatenate([jnp.where(comp == c, parts, 0.0) for c in range(COMPS)], 0)
         rows = COMPS * RHS
@@ -212,7 +201,6 @@
                 halves.append(half)
             dense[to] = jnp.concatenate(halves, 0)
 
-    with jax.named_scope("corner_send"):
         pl.semaphore_wait(far_sem, 2)
         order = sorted(range(1, nz), key=lambda d: -min(d, nz - d))
         copies_z = {}
@@ -226,24 +214,9 @@
                 device_id_type=MESH,
             )
             copies_z[d].start()
-
-    def selected(f, received):
-        received = received.astype(F32)
-        slots = [received[p * HALF : (p + 1) * HALF] for p in range(SUBS)]
-        values = []
-        for s in range(SUBS):
-            value = slots[0]
-            for p in range(1, SUBS):
-                value = jnp.where(partner[s, f] == p, slots[p], value)
-            values.append(value)
-        values = jnp.concatenate(values, 0)
-        return jnp.where(inside[f], values, 0.0)
-
-    none = jnp.zeros((HALF, width), F32)
-    visc_rows = jnp.concatenate([jnp.full((HALF, width), visc[s], F32) for s in range(SUBS)], 0)
-    size = SUBS * HALF
-
-    copies2 = []
+        return copies_z
+
+    copies2, corner_parts = [], []
     for c in range(2):
         with jax.named_scope(f"wait_traces{c}"):
             for f in range(4):
@@ -257,6 +230,11 @@
             below = jnp.concatenate([none, top[:-HALF]], 0)
             jump[4 * size : 5 * size] = (top - above).astype(BF16)
             jump[5 * size : 6 * size] = (bottom - below).astype(BF16)
+            pairs = nt_dot(jump[...], w_hi[...]) + nt_dot(jump[...], w_lo[...])
+            corner_parts.append(corner_values(pairs))
+            if c == 1:
+                with jax.named_scope("corners"):
+                    copies_z = send_corners(jnp.concatenate(corner_parts, 0))
             w_c[...] = jnp.dot(jump[...], c_mat[...], preferred_element_type=F32)
             w_s[...] = jnp.dot(jump[...], s_mat[...], preferred_element_type=F32)
             w_o[...] = jnp.dot(jump[...], o_mat[...], preferred_element_type=F32)
@@ -326,7 +304,7 @@
     finish(1)
 
     with jax.named_scope("sent"):
-        for copy in [*copies1[0], *copies1[1], *copies_y, *copies_z.values(), *copies_q, *copies2[0], *copies2[1]]:
+        for copy in [*copies1[0], *copies1[1], *copies_z.values(), *copies_q, *copies2[0], *copies2[1]]:
             copy.wait_send()
 
 
@@ -336,6 +314,11 @@
     nz = ny // QUAD
     vmem, dma = pltpu.VMEM, pltpu.SemaphoreType.DMA
     size = SUBS * HALF
+    inputs = (
+        traces, viscosity, partner, corner_owner, self_block, opposite_block, cross_block,
+        jnp.transpose(corner_map, (1, 0, 2)),
+    )
+    inputs = [pltpu.with_memory_space_constraint(value, pltpu.HBM) for value in inputs]
     applied, coarse = pl.pallas_call(
         functools.partial(kernel, nx, ny),
         out_shape=(
@@ -362,11 +345,8 @@
             vmem((6 * size, width), F32),
             vmem((2, 6, size, width), BF16),
             vmem((2, 4, size, width), BF16),
-            vmem((6 * BLOCK, width), BF16),
-            vmem((6 * BLOCK, width), BF16),
-            vmem((SUBS, 6, RHS, 6 * BLOCK), F32),
-            vmem((4, RHS, 128), F32),
-            vmem((4, RHS, 128), F32),
+            vmem((8 * BLOCK, width), BF16),
+            vmem((8 * BLOCK, width), BF16),
             vmem((nz, 16, 128), F32),
             vmem((nz, 16, 128), F32),
             vmem((16, 128), F32),
@@ -376,8 +356,6 @@
             dma((2, 4)),
             dma((2, 4)),
             dma((2, 4)),
-            dma((4,)),
-            dma((4,)),
             dma((nz,)),
             dma((nz,)),
             dma((QUAD,)),
@@ -387,7 +365,7 @@
         compiler_params=pltpu.CompilerParams(
             collective_id=0, has_side_effects=True, vmem_limit_bytes=40 * 2**20
         ),
-    )(traces, viscosity, partner, corner_owner, self_block, opposite_block, cross_block, jnp.transpose(corner_map, (1, 0, 2)))
+    )(*inputs)
     return applied, coarse[:, :8]
 
 

time: 51.7 us -> 44 us (0.85)
  local copies, waits for them, and re-layouts: 9.49 us -> 1.67 us
    unnamed x18 -> x2, local copies, waits for them, and re-layouts: 9.49 us -> 1.67 us
where the time goes in v2:
time: 44 us; the launch traced here: 43.6 us
  Pallas kernels  41.3 us (94%)
  local copies, waits for them, and re-layouts  1.67 us (4%)
  between operations  0.64 us (1%)
    pallas_call x1, Pallas kernels, body(): pl.pallas_call(functools.partial(kernel, nx, ny), out_shape=(jax.ShapeDty...  41.3 us
    unnamed x2, local copies, waits for them, and re-layouts  1.67 us

profile of v2, /device:TPU:1, one launch (start us, length us, event | category | flops | bytes accessed | tf_op | source)
XLA Modules:
  0.0 43.6 jit_solution(14935195710879479385)
XLA Ops:
  0.6 41.3 %shard_map.95 = (f32[1,1,4,6,16,768]{5,4,3,2,1,0:T(8,128)S(1)}, f32[48,128]{1,0:T(8,128)S(1)}) custom-call(bf16[1,1,4,6,16,768]{5,4,3,2,1,0:T(8,128)(2,1)} %traces.1, f32[1,1,4]{2,1,0:T(1,128)} %visc_in.1, s32[1,1,4,4]{3,2,1,0:T(4,128)} %partner_in.1, s32[1,1,4,8]{3,2,1,0:T(4,128)} %owner_in.1, bf16[768,768]{1,0:T(8,128)(2,1)} %self_in.1, ...), custom_call_target="tpu_custom_call" | custom-call | tf_op jit(solution)/shard_map/pallas_call | solution.py:322
  41.9 0.7 %copy.10 = f32[48,8]{0,1:T(8,128)} copy(f32[48,8]{1,0:T(8,128)S(1)} %bitcast.2) | data formatting | bytes 3072
  42.6 1.0 %copy.12 = f32[1,1,4,6,16,768]{5,4,3,2,1,0:T(8,128)} copy(f32[1,1,4,6,16,768]{5,4,3,2,1,0:T(8,128)S(1)} %get-tuple-element.10) | data formatting | bytes 2359296

commit v3 on v1

--- a/solution.py
+++ b/solution.py
@@ -44,7 +44,6 @@
 ):
     width = raw.shape[-1]
     nz = ny // QUAD
-    reach = nz // 4
     sx, sy = lax.axis_index("sx"), lax.axis_index("sy")
     z, quad = sy // QUAD, lax.rem(sy, QUAD)
 
@@ -59,13 +58,19 @@
     )
     inside = (sx < nx - 1, sx > 0, sy < ny - 1, sy > 0)
     quads = [(sx, z * QUAD + lax.rem(quad + j, QUAD)) for j in range(1, QUAD)]
-    near = [in_row(sy + QUAD * d) for d in range(1, reach + 1)]
-    near += [in_row(sy - QUAD * d) for d in range(1, reach + 1)]
 
     barrier = pltpu.get_barrier_semaphore()
-    greeted = [*beside, *quads, *near]
-    for device in greeted:
-        pl.semaphore_signal(barrier, inc=1, device_id=device, device_id_type=MESH)
+
+    def signal(semaphore, device):
+        pl.semaphore_signal(semaphore, inc=1, device_id=device, device_id_type=MESH)
+
+    with jax.named_scope("greet"):
+        for f in range(4):
+            pl.when(inside[f])(functools.partial(signal, barrier, beside[f]))
+        for device in quads:
+            signal(barrier, device)
+        for d in range(1, nz):
+            pl.when(z + d < nz)(functools.partial(signal, barrier, in_row(sy + QUAD * d)))
 
     loads = {}
     for i, (name, source, target) in enumerate((
@@ -90,11 +95,56 @@
             device_id=beside[f],
             device_id_type=MESH,
         )
-        copy.start()
-        return copy
+        pl.when(inside[f])(copy.start)
+        return (
+            lambda: pl.when(inside[OPP[f]])(copy.wait_recv),
+            lambda: pl.when(inside[f])(copy.wait_send),
+        )
+
+    lane = lax.broadcasted_iota(jnp.int32, (1, 128), 1)
+    block = lane // BLOCK
+
+    def moved(value, shift):
+        shift = (shift * BLOCK) % 128
+        return pltpu.roll(value, shift, 1) if shift else value
+
+    with jax.named_scope("weights"):
+        loads["cmap"].wait()
+        pad = jnp.zeros((BLOCK - KEYS, width), F32)
+        faces = [jnp.concatenate([cmap[f].astype(F32), pad], 0) for f in range(6)]
+        straight = jnp.concatenate(faces, 0).astype(BF16)
+        products = []
+        for name, matrix in (("cross", c_mat), ("self", s_mat), ("opp", o_mat)):
+            loads[name].wait()
+            product = nt_dot(straight, matrix[...])
+            products.append([product[f * BLOCK : (f + 1) * BLOCK] for f in range(6)])
+        cross, same, across = products
+        pairs = [cross[0] + cross[1], cross[2] + cross[3], cross[4] + cross[5]]
+        adjacent = [pairs[1] + pairs[2], pairs[0] + pairs[2], pairs[0] + pairs[1]]
+        weight = [same[f] + across[OPP[f]] + adjacent[f // 2] for f in range(6)]
+        weight.append(jnp.zeros((2 * BLOCK, width), F32))
+        w_hi[...], w_lo[...] = split(jnp.concatenate(weight, 0), 2)
+
+    def value_of(s, f, face, to):
+        tile = y_all[s, f, :, face // 4 * 128 : face // 4 * 128 + 128]
+        return jnp.where(block == to, moved(tile, to - face % 4), 0.0)
+
+    with jax.named_scope("values"):
+        loads["raw"].wait()
+        flat = raw[...].reshape(SUBS * 6 * RHS, width)
+        both = nt_dot(flat, w_hi[...]) + nt_dot(flat, w_lo[...])
+        y_all[...] = both.reshape(SUBS, 6, RHS, 8 * BLOCK)
+        for f in range(4):
+            y_out[f] = sum(value_of(s, f, OPP[f], s) for s in range(SUBS))
+
+    with jax.named_scope("entry"):
+        pl.semaphore_wait(barrier, sum(here.astype(jnp.int32) for here in inside) + len(quads) + z)
+
+    copies_y = [exchange(y_out.at[f], y_in, send_y, recv_y, f) for f in range(4)]
+    for d in range(1, nz):
+        pl.when(z >= d)(functools.partial(signal, far_sem, in_row(sy - QUAD * d)))
 
     with jax.named_scope("repack"):
-        loads["raw"].wait()
         for f in range(6):
             for s in range(SUBS):
                 both = raw[s, f].astype(F32)
@@ -104,70 +154,23 @@
                 for c in range(2):
                     out1[c, f] = own[c, f].reshape(SUBS * HALF, width).astype(BF16)
 
-    with jax.named_scope("entry"):
-        pl.semaphore_wait(barrier, len(greeted))
-
-    copies1 = [[exchange(out1.at[0, f], in1.at[0], send1.at[0], recv1.at[0], f) for f in range(4)]]
-    for device in (in_row(sy + QUAD * reach), in_row(sy - QUAD * reach)):
-        pl.semaphore_signal(far_sem, inc=1, device_id=device, device_id_type=MESH)
-
-    lane = lax.broadcasted_iota(jnp.int32, (1, 128), 1)
-    block = lane // BLOCK
-
-    def moved(value, shift):
-        shift = (shift * BLOCK) % 128
-        return pltpu.roll(value, shift, 1) if shift else value
-
-    with jax.named_scope("weights"):
-        loads["cmap"].wait()
-        pad = jnp.zeros((BLOCK - KEYS, width), F32)
-        faces = [jnp.concatenate([cmap[f].astype(F32), pad], 0) for f in range(6)]
-        pairs = [faces[0] + faces[1], faces[2] + faces[3], faces[4] + faces[5]]
-        adjacent = [pairs[1] + pairs[2], pairs[0] + pairs[2], pairs[0] + pairs[1]]
-        adjacent = jnp.concatenate([adjacent[f // 2] for f in range(6)], 0)
-        adj_hi, adj_lo = split(adjacent, 2)
-        straight = jnp.concatenate(faces, 0).astype(BF16)
-        flipped = jnp.concatenate([faces[OPP[f]] for f in range(6)], 0).astype(BF16)
-        loads["cross"].wait()
-        weight = nt_dot(adj_hi, c_mat[...]) + nt_dot(adj_lo, c_mat[...])
-        loads["self"].wait()
-        weight += nt_dot(straight, s_mat[...])
-        loads["opp"].wait()
-        weight += nt_dot(flipped, o_mat[...])
-        w_hi[...], w_lo[...] = split(weight, 2)
-
-    with jax.named_scope("corner_values"):
-        flat = raw[...].reshape(SUBS * 6 * RHS, width)
-        both = nt_dot(flat, w_hi[...]) + nt_dot(flat, w_lo[...])
-        y_all[...] = both.reshape(SUBS, 6, RHS, 6 * BLOCK)
-
-        def value_of(s, f, face, to):
-            if face < 4:
-                tile, at = y_all[s, f, :, :128], face
-            else:
-                tile = y_all[s, f, :, 128:]
-                tile = jnp.concatenate([tile, jnp.zeros((RHS, 64), F32)], 1)
-                at = face - 4
-            return jnp.where(block == to, moved(tile, to - at), 0.0)
-
-        copies_y = []
-        for f in range(4):
-            y_out[f] = sum(value_of(s, f, OPP[f], s) for s in range(SUBS))
-            copies_y.append(exchange(y_out.at[f], y_in, send_y, recv_y, f))
-
-    copies1.append([exchange(out1.at[1, f], in1.at[1], send1.at[1], recv1.at[1], f) for f in range(4)])
-
-    with jax.named_scope("own_corners"):
+    copies1 = [
+        [exchange(out1.at[c, f], in1.at[c], send1.at[c], recv1.at[c], f) for f in range(4)]
+        for c in range(2)
+    ]
+
+    for f in range(4):
+        def clear(f=f):
+            y_in[f] = jnp.zeros(y_in.shape[1:], F32)
+            for ref in (in1, in2):
+                for c in range(2):
+                    ref[c, f] = jnp.zeros(ref.shape[2:], BF16)
+
+        pl.when(jnp.logical_not(inside[f]))(clear)
+
+    with jax.named_scope("owners"):
         for name in ("visc", "partner", "owner"):
             loads[name].wait()
-        parts = jnp.zeros((RHS, 128), F32)
-        for s in range(SUBS):
-            for f in range(6):
-                parts += value_of(s, f, f, s)
-            if s < SUBS - 1:
-                parts -= value_of(s + 1, 5, 4, s)
-            if s > 0:
-                parts -= value_of(s - 1, 4, 5, s)
         visc_lanes = jnp.zeros((1, 128), F32)
         for s in range(SUBS):
             visc_lanes = jnp.where(block == s, visc[s], visc_lanes)
@@ -179,20 +182,28 @@
                 owners = jnp.where((row >= first) & (row < first + COMPS), owner[s, m], owners)
         unknown = lax.broadcasted_iota(jnp.int32, (SUBS * BLOCK, 8 * ny), 1)
         onehot = jnp.where(unknown == owners, 1.0, 0.0).astype(BF16)
+        parts = jnp.zeros((RHS, 128), F32)
+        for s in range(SUBS):
+            for f in range(6):
+                parts += value_of(s, f, f, s)
+            if s < SUBS - 1:
+                parts -= value_of(s + 1, 5, 4, s)
+            if s > 0:
+                parts -= value_of(s - 1, 4, 5, s)
+
+    with jax.named_scope("wait_values"):
+        for wait, _ in copies_y:
+            wait()
 
     with jax.named_scope("corners"):
-        for f in range(4):
-            copies_y[f].wait_recv()
         for f in range(4):
             received = y_in[f]
             slots = jnp.zeros((1, 128), jnp.int32)
             for s in range(SUBS):
                 slots = jnp.where(block == s, partner[s, f], slots)
-            chosen = jnp.zeros((RHS, 128), F32)
             for d in range(SUBS):
                 here = slots == lax.rem(block - d + SUBS, SUBS)
-                chosen += jnp.where(here, moved(received, d), 0.0)
-            parts -= jnp.where(inside[f], chosen, 0.0)
+                parts -= jnp.where(here, moved(received, d), 0.0)
         parts = parts * visc_lanes
         comp = lax.rem(lax.rem(lane, BLOCK), COMPS)
         stacked = jnp.concatenate([jnp.where(comp == c, parts, 0.0) for c in range(COMPS)], 0)
@@ -210,22 +221,21 @@
                     value = moved(tiles[g * 8 : g * 8 + 8], g % 4 - to % 4)
                     half = jnp.where(block == g % 4, value, half)
                 halves.append(half)
-            dense[to] = jnp.concatenate(halves, 0)
-
-    with jax.named_scope("corner_send"):
-        pl.semaphore_wait(far_sem, 2)
-        order = sorted(range(1, nz), key=lambda d: -min(d, nz - d))
-        copies_z = {}
-        for d in order:
-            copies_z[d] = pltpu.make_async_remote_copy(
-                src_ref=dense.at[lax.rem(z + d, nz)],
-                dst_ref=z_in.at[d],
-                send_sem=send_z.at[d],
-                recv_sem=recv_z.at[d],
-                device_id=in_row(sy + QUAD * d),
-                device_id_type=MESH,
-            )
-            copies_z[d].start()
+            dense[to, :8] = halves[0]
+            dense[to, 8:] = jnp.where(block < 2, halves[1][:4], moved(halves[1][4:], 2))
+
+    order = sorted(range(1, nz), key=lambda d: -min(d, nz - d))
+    copies_z = {}
+    for d in order:
+        copies_z[d] = pltpu.make_async_remote_copy(
+            src_ref=dense.at[lax.rem(z + d, nz)],
+            dst_ref=z_in.at[d],
+            send_sem=send_z.at[d],
+            recv_sem=recv_z.at[d],
+            device_id=in_row(sy + QUAD * d),
+            device_id_type=MESH,
+        )
+        pl.when(z + d >= nz)(copies_z[d].start)
 
     def selected(f, received):
         received = received.astype(F32)
@@ -236,8 +246,7 @@
             for p in range(1, SUBS):
                 value = jnp.where(partner[s, f] == p, slots[p], value)
             values.append(value)
-        values = jnp.concatenate(values, 0)
-        return jnp.where(inside[f], values, 0.0)
+        return jnp.concatenate(values, 0)
 
     none = jnp.zeros((HALF, width), F32)
     visc_rows = jnp.concatenate([jnp.full((HALF, width), visc[s], F32) for s in range(SUBS)], 0)
@@ -246,8 +255,8 @@
     copies2 = []
     for c in range(2):
         with jax.named_scope(f"wait_traces{c}"):
-            for f in range(4):
-                copies1[c][f].wait_recv()
+            for wait, _ in copies1[c]:
+                wait()
         with jax.named_scope(f"local{c}"):
             for f in range(4):
                 mine = own[c, f].reshape(size, width)
@@ -283,18 +292,29 @@
 
     def finish(c):
         with jax.named_scope(f"wait_local{c}"):
-            for f in range(4):
-                copies2[c][f].wait_recv()
+            for wait, _ in copies2[c]:
+                wait()
         with jax.named_scope(f"applied{c}"):
             for f in range(4):
                 value = local[c, f].astype(F32) - selected(f, in2[c, f])
                 for s in range(SUBS):
                     applied[0, 0, s, f, c * HALF : (c + 1) * HALF] = value[s * HALF : (s + 1) * HALF]
 
+    with jax.named_scope("far"):
+        pl.when(z < nz - 1)(lambda: pl.semaphore_wait(far_sem, nz - 1 - z))
+        for d in order:
+            pl.when(z + d < nz)(copies_z[d].start)
+
+    finish(0)
+    finish(1)
+
     with jax.named_scope("corner_sum"):
+        mine = dense[0]
+        for at in range(1, nz):
+            mine = jnp.where(z == at, dense[at], mine)
         for d in range(1, nz):
             copies_z[d].wait_recv()
-        values = [dense[z]] + [z_in[d] for d in range(1, nz)]
+        values = [mine] + [z_in[d] for d in range(1, nz)]
         while len(values) > 1:
             values = [a + b for a, b in zip(values[::2], values[1::2])] + values[len(values) & ~1 :]
         quad_out[...] = values[0]
@@ -310,8 +330,6 @@
             ))
             copies_q[-1].start()
 
-    finish(0)
-
     with jax.named_scope("corner_end"):
         for copy in copies_q:
             copy.wait_recv()
@@ -319,15 +337,16 @@
         mine = result
         for j in range(1, QUAD):
             mine = jnp.where(quad == j, pltpu.roll(result, 128 - 8 * j, 1), mine)
+        low = mine[8:]
+        tiles = (mine[:8], jnp.concatenate([low, moved(low, -2)], 0))
         for g in range(6):
-            value = moved(mine[g // 4 * 8 : g // 4 * 8 + 8], -(g % 4))
-            coarse[pl.ds(g % 2 * HALF * COMPS + g // 2, HALF, stride=COMPS)] = value
-
-    finish(1)
+            coarse[pl.ds(g % 2 * HALF * COMPS + g // 2, HALF, stride=COMPS)] = moved(tiles[g // 4], -(g % 4))
 
     with jax.named_scope("sent"):
-        for copy in [*copies1[0], *copies1[1], *copies_y, *copies_z.values(), *copies_q, *copies2[0], *copies2[1]]:
+        for copy in [*copies_z.values(), *copies_q]:
             copy.wait_send()
+        for _, wait in [*copies_y, *copies1[0], *copies1[1], *copies2[0], *copies2[1]]:
+            wait()
 
 
 def body(traces, viscosity, partner, corner_owner, self_block, opposite_block, cross_block, corner_map):
@@ -336,6 +355,11 @@
     nz = ny // QUAD
     vmem, dma = pltpu.VMEM, pltpu.SemaphoreType.DMA
     size = SUBS * HALF
+    inputs = (
+        traces, viscosity, partner, corner_owner, self_block, opposite_block, cross_block,
+        jnp.transpose(corner_map, (1, 0, 2)),
+    )
+    inputs = [pltpu.with_memory_space_constraint(value, pltpu.HBM) for value in inputs]
     applied, coarse = pl.pallas_call(
         functools.partial(kernel, nx, ny),
         out_shape=(
@@ -362,15 +386,15 @@
             vmem((6 * size, width), F32),
             vmem((2, 6, size, width), BF16),
             vmem((2, 4, size, width), BF16),
-            vmem((6 * BLOCK, width), BF16),
-            vmem((6 * BLOCK, width), BF16),
-            vmem((SUBS, 6, RHS, 6 * BLOCK), F32),
+            vmem((8 * BLOCK, width), BF16),
+            vmem((8 * BLOCK, width), BF16),
+            vmem((SUBS, 6, RHS, 8 * BLOCK), F32),
             vmem((4, RHS, 128), F32),
             vmem((4, RHS, 128), F32),
-            vmem((nz, 16, 128), F32),
-            vmem((nz, 16, 128), F32),
-            vmem((16, 128), F32),
-            vmem((QUAD, 16, 128), F32),
+            vmem((nz, 12, 128), F32),
+            vmem((nz, 12, 128), F32),
+            vmem((12, 128), F32),
+            vmem((QUAD, 12, 128), F32),
             dma((8,)),
             dma((2, 4)),
             dma((2, 4)),
@@ -387,7 +411,7 @@
         compiler_params=pltpu.CompilerParams(
             collective_id=0, has_side_effects=True, vmem_limit_bytes=40 * 2**20
         ),
-    )(traces, viscosity, partner, corner_owner, self_block, opposite_block, cross_block, jnp.transpose(corner_map, (1, 0, 2)))
+    )(*inputs)
     return applied, coarse[:, :8]
 
 

time: 51.7 us -> 39.5 us (0.76)
  the two profiles are of different devices: /device:TPU:1 before, /device:TPU:43 now
where the time goes in v3:
time: 39.5 us; the launch traced here: 39.4 us
  Pallas kernels  37.1 us (94%)
  local copies, waits for them, and re-layouts  1.67 us (4%)
  between operations  0.64 us (2%)
    pallas_call x1, Pallas kernels, body(): pl.pallas_call(functools.partial(kernel, nx, ny), out_shape=(jax.ShapeDty...  37.1 us
    unnamed x2, local copies, waits for them, and re-layouts  1.67 us

profile of v3, /device:TPU:43, one launch (start us, length us, event | category | flops | bytes accessed | tf_op | source)
XLA Modules:
  0.0 39.4 jit_solution(4731407443932774668)
XLA Ops:
  0.6 37.1 %shard_map.95 = (f32[1,1,4,6,16,768]{5,4,3,2,1,0:T(8,128)S(1)}, f32[48,128]{1,0:T(8,128)S(1)}) custom-call(bf16[1,1,4,6,16,768]{5,4,3,2,1,0:T(8,128)(2,1)} %traces.1, f32[1,1,4]{2,1,0:T(1,128)} %visc_in.1, s32[1,1,4,4]{3,2,1,0:T(4,128)} %partner_in.1, s32[1,1,4,8]{3,2,1,0:T(4,128)} %owner_in.1, bf16[768,768]{1,0:T(8,128)(2,1)} %self_in.1, ...), custom_call_target="tpu_custom_call" | custom-call | tf_op jit(solution)/shard_map/pallas_call | solution.py:363
  37.7 0.7 %copy.10 = f32[48,8]{0,1:T(8,128)} copy(f32[48,8]{1,0:T(8,128)S(1)} %bitcast.2) | data formatting | bytes 3072
  38.4 1.0 %copy.12 = f32[1,1,4,6,16,768]{5,4,3,2,1,0:T(8,128)} copy(f32[1,1,4,6,16,768]{5,4,3,2,1,0:T(8,128)S(1)} %get-tuple-element.10) | data formatting | bytes 2359296

commit v4 on v3

--- a/solution.py
+++ b/solution.py
@@ -39,13 +39,12 @@
     applied, coarse,
     raw, s_mat, o_mat, c_mat, cmap, visc, partner, owner,
     own, out1, in1, jump, w_s, w_o, w_c, local, in2,
-    w_hi, w_lo, y_all, y_out, y_in, dense, z_in, quad_out, quad_in,
-    load_sem, send1, recv1, send2, recv2, send_y, recv_y, send_z, recv_z, send_q, recv_q, far_sem,
+    w_hi, w_lo, y_all, y_out, y_in, stacked, dense, z_in,
+    load_sem, send1, recv1, send2, recv2, send_y, recv_y, send_z, recv_z, far_sem,
 ):
     width = raw.shape[-1]
-    nz = ny // QUAD
     sx, sy = lax.axis_index("sx"), lax.axis_index("sy")
-    z, quad = sy // QUAD, lax.rem(sy, QUAD)
+    z = sy // QUAD
 
     def in_row(to):
         return (sx, lax.rem(to + ny, ny))
@@ -57,7 +56,6 @@
         in_row(sy - 1),
     )
     inside = (sx < nx - 1, sx > 0, sy < ny - 1, sy > 0)
-    quads = [(sx, z * QUAD + lax.rem(quad + j, QUAD)) for j in range(1, QUAD)]
 
     barrier = pltpu.get_barrier_semaphore()
 
@@ -67,10 +65,6 @@
     with jax.named_scope("greet"):
         for f in range(4):
             pl.when(inside[f])(functools.partial(signal, barrier, beside[f]))
-        for device in quads:
-            signal(barrier, device)
-        for d in range(1, nz):
-            pl.when(z + d < nz)(functools.partial(signal, barrier, in_row(sy + QUAD * d)))
 
     loads = {}
     for i, (name, source, target) in enumerate((
@@ -85,6 +79,16 @@
     )):
         loads[name] = pltpu.make_async_copy(source, target, load_sem.at[i])
         loads[name].start()
+
+    known = (z + 1) * QUAD
+
+    def to_others(first, last, act):
+        @pl.loop(first, last)
+        def _(to):
+            pl.when(to != sy)(lambda: act(to))
+
+    with jax.named_scope("greet_row"):
+        to_others(z * QUAD, ny, lambda to: signal(barrier, (sx, to)))
 
     def exchange(source, target, sends, recvs, f):
         copy = pltpu.make_async_remote_copy(
@@ -138,12 +142,9 @@
             y_out[f] = sum(value_of(s, f, OPP[f], s) for s in range(SUBS))
 
     with jax.named_scope("entry"):
-        pl.semaphore_wait(barrier, sum(here.astype(jnp.int32) for here in inside) + len(quads) + z)
+        pl.semaphore_wait(barrier, sum(here.astype(jnp.int32) for here in inside) + known - 1)
 
     copies_y = [exchange(y_out.at[f], y_in, send_y, recv_y, f) for f in range(4)]
-    for d in range(1, nz):
-        pl.when(z >= d)(functools.partial(signal, far_sem, in_row(sy - QUAD * d)))
-
     with jax.named_scope("repack"):
         for f in range(6):
             for s in range(SUBS):
@@ -159,6 +160,8 @@
         for c in range(2)
     ]
 
+    to_others(0, z * QUAD, lambda to: signal(far_sem, (sx, to)))
+
     for f in range(4):
         def clear(f=f):
             y_in[f] = jnp.zeros(y_in.shape[1:], F32)
@@ -174,13 +177,12 @@
         visc_lanes = jnp.zeros((1, 128), F32)
         for s in range(SUBS):
             visc_lanes = jnp.where(block == s, visc[s], visc_lanes)
-        row = lax.broadcasted_iota(jnp.int32, (SUBS * BLOCK, 1), 0)
-        owners = jnp.full((SUBS * BLOCK, 1), -1, jnp.int32)
+        owners = jnp.full((1, 128), -1, jnp.int32)
         for s in range(SUBS):
             for m in range(CORNERS):
                 first = s * BLOCK + m * COMPS
-                owners = jnp.where((row >= first) & (row < first + COMPS), owner[s, m], owners)
-        unknown = lax.broadcasted_iota(jnp.int32, (SUBS * BLOCK, 8 * ny), 1)
+                owners = jnp.where((lane >= first) & (lane < first + COMPS), owner[s, m], owners)
+        unknown = lax.broadcasted_iota(jnp.int32, (8 * ny, 1), 0)
         onehot = jnp.where(unknown == owners, 1.0, 0.0).astype(BF16)
         parts = jnp.zeros((RHS, 128), F32)
         for s in range(SUBS):
@@ -206,36 +208,38 @@
                 parts -= jnp.where(here, moved(received, d), 0.0)
         parts = parts * visc_lanes
         comp = lax.rem(lax.rem(lane, BLOCK), COMPS)
-        stacked = jnp.concatenate([jnp.where(comp == c, parts, 0.0) for c in range(COMPS)], 0)
-        rows = COMPS * RHS
-        total = jnp.dot(
-            jnp.concatenate(split(stacked, 3), 0), onehot, preferred_element_type=F32
-        )
-        total = total[:rows] + total[rows : 2 * rows] + total[2 * rows :]
-        for to in range(nz):
-            tiles = total[:, to // 4 * 128 : to // 4 * 128 + 128]
-            halves = []
-            for groups in ((0, 1, 2, 3), (4, 5)):
-                half = jnp.zeros((8, 128), F32)
-                for g in groups:
-                    value = moved(tiles[g * 8 : g * 8 + 8], g % 4 - to % 4)
-                    half = jnp.where(block == g % 4, value, half)
-                halves.append(half)
-            dense[to, :8] = halves[0]
-            dense[to, 8:] = jnp.where(block < 2, halves[1][:4], moved(halves[1][4:], 2))
-
-    order = sorted(range(1, nz), key=lambda d: -min(d, nz - d))
-    copies_z = {}
-    for d in order:
-        copies_z[d] = pltpu.make_async_remote_copy(
-            src_ref=dense.at[lax.rem(z + d, nz)],
-            dst_ref=z_in.at[d],
-            send_sem=send_z.at[d],
-            recv_sem=recv_z.at[d],
-            device_id=in_row(sy + QUAD * d),
+        for c in range(COMPS):
+            stacked[pl.ds(c, RHS, stride=COMPS)] = jnp.where(comp == c, parts, 0.0)
+        pieces = split(stacked[...], 3)
+        total = sum(nt_dot(onehot, piece) for piece in pieces)
+        total = total.reshape(ny, 8, RHS * COMPS)
+        total = jnp.concatenate([total, jnp.zeros((ny, 8, 128 - RHS * COMPS), F32)], 2)
+        for to in range(ny):
+            tile = total[to]
+            dense[to] = jnp.where(lane < 64, tile[:4], pltpu.roll(tile[4:], 64, 1))
+
+    def corner_copy(to):
+        return pltpu.make_async_remote_copy(
+            src_ref=dense.at[to],
+            dst_ref=z_in.at[sy],
+            send_sem=send_z.at[to],
+            recv_sem=recv_z.at[sy],
+            device_id=(sx, to),
             device_id_type=MESH,
         )
-        pl.when(z + d >= nz)(copies_z[d].start)
+
+    def corner_arrival(source):
+        return pltpu.make_async_remote_copy(
+            src_ref=dense.at[source],
+            dst_ref=z_in.at[source],
+            send_sem=send_z.at[source],
+            recv_sem=recv_z.at[source],
+            device_id=(sx, source),
+            device_id_type=MESH,
+        )
+
+    with jax.named_scope("corner_send"):
+        to_others(0, known, lambda to: corner_copy(to).start())
 
     def selected(f, received):
         received = received.astype(F32)
@@ -301,50 +305,23 @@
                     applied[0, 0, s, f, c * HALF : (c + 1) * HALF] = value[s * HALF : (s + 1) * HALF]
 
     with jax.named_scope("far"):
-        pl.when(z < nz - 1)(lambda: pl.semaphore_wait(far_sem, nz - 1 - z))
-        for d in order:
-            pl.when(z + d < nz)(copies_z[d].start)
+        pl.when(known < ny)(lambda: pl.semaphore_wait(far_sem, ny - known))
+        to_others(known, ny, lambda to: corner_copy(to).start())
 
     finish(0)
     finish(1)
 
+    with jax.named_scope("corner_wait"):
+        to_others(0, ny, lambda source: corner_arrival(source).wait_recv())
     with jax.named_scope("corner_sum"):
-        mine = dense[0]
-        for at in range(1, nz):
-            mine = jnp.where(z == at, dense[at], mine)
-        for d in range(1, nz):
-            copies_z[d].wait_recv()
-        values = [mine] + [z_in[d] for d in range(1, nz)]
-        while len(values) > 1:
-            values = [a + b for a, b in zip(values[::2], values[1::2])] + values[len(values) & ~1 :]
-        quad_out[...] = values[0]
-        copies_q = []
-        for j in range(1, QUAD):
-            copies_q.append(pltpu.make_async_remote_copy(
-                src_ref=quad_out,
-                dst_ref=quad_in.at[j],
-                send_sem=send_q.at[j],
-                recv_sem=recv_q.at[j],
-                device_id=quads[j - 1],
-                device_id_type=MESH,
-            ))
-            copies_q[-1].start()
-
-    with jax.named_scope("corner_end"):
-        for copy in copies_q:
-            copy.wait_recv()
-        result = (quad_out[...] + quad_in[1]) + (quad_in[2] + quad_in[3])
-        mine = result
-        for j in range(1, QUAD):
-            mine = jnp.where(quad == j, pltpu.roll(result, 128 - 8 * j, 1), mine)
-        low = mine[8:]
-        tiles = (mine[:8], jnp.concatenate([low, moved(low, -2)], 0))
-        for g in range(6):
-            coarse[pl.ds(g % 2 * HALF * COMPS + g // 2, HALF, stride=COMPS)] = moved(tiles[g // 4], -(g % 4))
+        result = jnp.zeros((4, 128), F32)
+        for source in range(ny):
+            result += jnp.where(sy == source, dense[source], z_in[source])
+        coarse[:4] = result
+        coarse[4:] = pltpu.roll(result, 64, 1)
 
     with jax.named_scope("sent"):
-        for copy in [*copies_z.values(), *copies_q]:
-            copy.wait_send()
+        to_others(0, ny, lambda to: corner_copy(to).wait_send())
         for _, wait in [*copies_y, *copies1[0], *copies1[1], *copies2[0], *copies2[1]]:
             wait()
 
@@ -352,7 +329,6 @@
 def body(traces, viscosity, partner, corner_owner, self_block, opposite_block, cross_block, corner_map):
     nx, ny = lax.axis_size("sx"), lax.axis_size("sy")
     width = traces.shape[-1]
-    nz = ny // QUAD
     vmem, dma = pltpu.VMEM, pltpu.SemaphoreType.DMA
     size = SUBS * HALF
     inputs = (
@@ -364,7 +340,7 @@
         functools.partial(kernel, nx, ny),
         out_shape=(
             jax.ShapeDtypeStruct(traces.shape, F32),
-            jax.ShapeDtypeStruct((RHS * COMPS, 128), F32),
+            jax.ShapeDtypeStruct((8, 128), F32),
         ),
         in_specs=[pl.BlockSpec(memory_space=pltpu.HBM)] * 8,
         out_specs=(pl.BlockSpec(memory_space=vmem), pl.BlockSpec(memory_space=vmem)),
@@ -391,10 +367,9 @@
             vmem((SUBS, 6, RHS, 8 * BLOCK), F32),
             vmem((4, RHS, 128), F32),
             vmem((4, RHS, 128), F32),
-            vmem((nz, 12, 128), F32),
-            vmem((nz, 12, 128), F32),
-            vmem((12, 128), F32),
-            vmem((QUAD, 12, 128), F32),
+            vmem((RHS * COMPS, 128), F32),
+            vmem((ny, 4, 128), F32),
+            vmem((ny, 4, 128), F32),
             dma((8,)),
             dma((2, 4)),
             dma((2, 4)),
@@ -402,17 +377,15 @@
             dma((2, 4)),
             dma((4,)),
             dma((4,)),
-            dma((nz,)),
-            dma((nz,)),
-            dma((QUAD,)),
-            dma((QUAD,)),
+            dma((ny,)),
+            dma((ny,)),
             pltpu.SemaphoreType.REGULAR,
         ],
         compiler_params=pltpu.CompilerParams(
             collective_id=0, has_side_effects=True, vmem_limit_bytes=40 * 2**20
         ),
     )(*inputs)
-    return applied, coarse[:, :8]
+    return applied, coarse[:, : RHS * COMPS].T
 
 
 def solution(mesh):

time: 39.5 us -> 37.9 us (0.959)
  the two profiles are of different devices: /device:TPU:43 before, /device:TPU:1 now
where the time goes in v4:
time: 37.9 us; the launch traced here: 37.7 us
  Pallas kernels  35.5 us (94%)
  local copies, waits for them, and re-layouts  1.61 us (4%)
  between operations  0.64 us (2%)
    pallas_call x1, Pallas kernels, body(): pl.pallas_call(functools.partial(kernel, nx, ny), out_shape=(jax.ShapeDty...  35.5 us
    unnamed x1, local copies, waits for them, and re-layouts  1.01 us

profile of v4, /device:TPU:1, one launch (start us, length us, event | category | flops | bytes accessed | tf_op | source)
XLA Modules:
  0.0 37.7 jit_solution(14634031128757689453)
XLA Ops:
  0.6 35.5 %shard_map.95 = (f32[1,1,4,6,16,768]{5,4,3,2,1,0:T(8,128)S(1)}, f32[8,128]{1,0:T(8,128)S(1)}) custom-call(bf16[1,1,4,6,16,768]{5,4,3,2,1,0:T(8,128)(2,1)} %traces.1, f32[1,1,4]{2,1,0:T(1,128)} %visc_in.1, s32[1,1,4,4]{3,2,1,0:T(4,128)} %partner_in.1, s32[1,1,4,8]{3,2,1,0:T(4,128)} %owner_in.1, bf16[768,768]{1,0:T(8,128)(2,1)} %self_in.1, ...), custom_call_target="tpu_custom_call" | custom-call | tf_op jit(solution)/shard_map/pallas_call | solution.py:339
  36.1 0.6 %slice_bitcast_fusion = f32[48,8]{0,1:T(8,128)} fusion(f32[8,128]{1,0:T(8,128)S(1)} %get-tuple-element.5), kind=kLoop, calls=%fused_computation | loop fusion | bytes 3072 | tf_op jit(solution)/shard_map/transpose | solution.py:388
  36.7 1.0 %copy.11 = f32[1,1,4,6,16,768]{5,4,3,2,1,0:T(8,128)} copy(f32[1,1,4,6,16,768]{5,4,3,2,1,0:T(8,128)S(1)} %get-tuple-element.8) | data formatting | bytes 2359296

commit v5 on v4

--- a/solution.py
+++ b/solution.py
@@ -18,6 +18,7 @@
 BLOCK = 32
 QUAD = 4
 OPP = (1, 0, 3, 2, 5, 4)
+FIRST = 4 * QUAD
 
 
 def nt_dot(left, right):
@@ -40,7 +41,7 @@
     raw, s_mat, o_mat, c_mat, cmap, visc, partner, owner,
     own, out1, in1, jump, w_s, w_o, w_c, local, in2,
     w_hi, w_lo, y_all, y_out, y_in, stacked, dense, z_in,
-    load_sem, send1, recv1, send2, recv2, send_y, recv_y, send_z, recv_z, far_sem,
+    load_sem, send, recv, share_sem, far_sem,
 ):
     width = raw.shape[-1]
     sx, sy = lax.axis_index("sx"), lax.axis_index("sy")
@@ -68,11 +69,11 @@
 
     loads = {}
     for i, (name, source, target) in enumerate((
-        ("raw", traces.at[0, 0], raw),
         ("cmap", cmap_in, cmap),
         ("cross", cross_in, c_mat),
         ("self", self_in, s_mat),
         ("opp", opp_in, o_mat),
+        ("raw", traces.at[0, 0], raw),
         ("visc", visc_in.at[0, 0], visc),
         ("partner", partner_in.at[0, 0], partner),
         ("owner", owner_in.at[0, 0], owner),
@@ -90,20 +91,46 @@
     with jax.named_scope("greet_row"):
         to_others(z * QUAD, ny, lambda to: signal(barrier, (sx, to)))
 
-    def exchange(source, target, sends, recvs, f):
+    count = sum(here.astype(jnp.int32) for here in inside)
+
+    def exchange(step, source, target, f):
         copy = pltpu.make_async_remote_copy(
-            src_ref=source,
+            src_ref=source.at[f],
             dst_ref=target.at[OPP[f]],
-            send_sem=sends.at[f],
-            recv_sem=recvs.at[OPP[f]],
+            send_sem=send.at[step],
+            recv_sem=recv.at[step],
             device_id=beside[f],
             device_id_type=MESH,
         )
         pl.when(inside[f])(copy.start)
-        return (
-            lambda: pl.when(inside[OPP[f]])(copy.wait_recv),
-            lambda: pl.when(inside[f])(copy.wait_send),
-        )
+
+    def arrival(step, source, target):
+        copies = [
+            pltpu.make_async_remote_copy(
+                src_ref=source.at[pl.ds(0, k)],
+                dst_ref=target.at[pl.ds(0, k)],
+                send_sem=send.at[step],
+                recv_sem=recv.at[step],
+                device_id=beside[0],
+                device_id_type=MESH,
+            )
+            for k in (2, 3, 4)
+        ]
+
+        def wait(which):
+            for k, copy in zip((2, 3, 4), copies):
+                pl.when(count == k)(getattr(copy, which))
+
+        return wait
+
+    steps = [
+        (0, y_out, y_in),
+        (1, out1.at[0], in1.at[0]),
+        (2, out1.at[1], in1.at[1]),
+        (3, local.at[0], in2.at[0]),
+        (4, local.at[1], in2.at[1]),
+    ]
+    arrivals = [arrival(*step) for step in steps]
 
     lane = lax.broadcasted_iota(jnp.int32, (1, 128), 1)
     block = lane // BLOCK
@@ -112,17 +139,23 @@
         shift = (shift * BLOCK) % 128
         return pltpu.roll(value, shift, 1) if shift else value
 
-    with jax.named_scope("weights"):
+    with jax.named_scope("corner_map"):
         loads["cmap"].wait()
         pad = jnp.zeros((BLOCK - KEYS, width), F32)
         faces = [jnp.concatenate([cmap[f].astype(F32), pad], 0) for f in range(6)]
         straight = jnp.concatenate(faces, 0).astype(BF16)
-        products = []
-        for name, matrix in (("cross", c_mat), ("self", s_mat), ("opp", o_mat)):
-            loads[name].wait()
-            product = nt_dot(straight, matrix[...])
-            products.append([product[f * BLOCK : (f + 1) * BLOCK] for f in range(6)])
-        cross, same, across = products
+
+    def through(name, matrix):
+        loads[name].wait()
+        product = nt_dot(straight, matrix[...])
+        return [product[f * BLOCK : (f + 1) * BLOCK] for f in range(6)]
+
+    with jax.named_scope("weights_cross"):
+        cross = through("cross", c_mat)
+    with jax.named_scope("weights_self"):
+        same = through("self", s_mat)
+    with jax.named_scope("weights_opposite"):
+        across = through("opp", o_mat)
         pairs = [cross[0] + cross[1], cross[2] + cross[3], cross[4] + cross[5]]
         adjacent = [pairs[1] + pairs[2], pairs[0] + pairs[2], pairs[0] + pairs[1]]
         weight = [same[f] + across[OPP[f]] + adjacent[f // 2] for f in range(6)]
@@ -133,18 +166,24 @@
         tile = y_all[s, f, :, face // 4 * 128 : face // 4 * 128 + 128]
         return jnp.where(block == to, moved(tile, to - face % 4), 0.0)
 
-    with jax.named_scope("values"):
-        loads["raw"].wait()
-        flat = raw[...].reshape(SUBS * 6 * RHS, width)
+    def values(f):
+        flat = raw[:, f : f + 2].reshape(SUBS * 2 * RHS, width)
         both = nt_dot(flat, w_hi[...]) + nt_dot(flat, w_lo[...])
-        y_all[...] = both.reshape(SUBS, 6, RHS, 8 * BLOCK)
-        for f in range(4):
-            y_out[f] = sum(value_of(s, f, OPP[f], s) for s in range(SUBS))
-
-    with jax.named_scope("entry"):
-        pl.semaphore_wait(barrier, sum(here.astype(jnp.int32) for here in inside) + known - 1)
-
-    copies_y = [exchange(y_out.at[f], y_in, send_y, recv_y, f) for f in range(4)]
+        y_all[:, f : f + 2] = both.reshape(SUBS, 2, RHS, 8 * BLOCK)
+
+    for f in (0, 2):
+        with jax.named_scope(f"values{f}"):
+            if f == 0:
+                loads["raw"].wait()
+            values(f)
+            for to in (f, f + 1):
+                y_out[to] = sum(value_of(s, to, OPP[to], s) for s in range(SUBS))
+        if f == 0:
+            with jax.named_scope("entry"):
+                pl.semaphore_wait(barrier, count + known - 1)
+        for to in (f, f + 1):
+            exchange(*steps[0], to)
+
     with jax.named_scope("repack"):
         for f in range(6):
             for s in range(SUBS):
@@ -155,11 +194,9 @@
                 for c in range(2):
                     out1[c, f] = own[c, f].reshape(SUBS * HALF, width).astype(BF16)
 
-    copies1 = [
-        [exchange(out1.at[c, f], in1.at[c], send1.at[c], recv1.at[c], f) for f in range(4)]
-        for c in range(2)
-    ]
-
+    for c in range(2):
+        for f in range(4):
+            exchange(*steps[1 + c], f)
     to_others(0, z * QUAD, lambda to: signal(far_sem, (sx, to)))
 
     for f in range(4):
@@ -184,6 +221,7 @@
                 owners = jnp.where((lane >= first) & (lane < first + COMPS), owner[s, m], owners)
         unknown = lax.broadcasted_iota(jnp.int32, (8 * ny, 1), 0)
         onehot = jnp.where(unknown == owners, 1.0, 0.0).astype(BF16)
+        values(4)
         parts = jnp.zeros((RHS, 128), F32)
         for s in range(SUBS):
             for f in range(6):
@@ -194,8 +232,7 @@
                 parts -= value_of(s - 1, 4, 5, s)
 
     with jax.named_scope("wait_values"):
-        for wait, _ in copies_y:
-            wait()
+        arrivals[0]("wait_recv")
 
     with jax.named_scope("corners"):
         for f in range(4):
@@ -211,35 +248,41 @@
         for c in range(COMPS):
             stacked[pl.ds(c, RHS, stride=COMPS)] = jnp.where(comp == c, parts, 0.0)
         pieces = split(stacked[...], 3)
-        total = sum(nt_dot(onehot, piece) for piece in pieces)
-        total = total.reshape(ny, 8, RHS * COMPS)
-        total = jnp.concatenate([total, jnp.zeros((ny, 8, 128 - RHS * COMPS), F32)], 2)
-        for to in range(ny):
-            tile = total[to]
+
+    def assemble(first, last):
+        total = sum(nt_dot(onehot[first * 8 : last * 8], piece) for piece in pieces)
+        total = total.reshape(last - first, 8, RHS * COMPS)
+        pad = jnp.zeros((last - first, 8, 128 - RHS * COMPS), F32)
+        total = jnp.concatenate([total, pad], 2)
+        for to in range(first, last):
+            tile = total[to - first]
             dense[to] = jnp.where(lane < 64, tile[:4], pltpu.roll(tile[4:], 64, 1))
 
     def corner_copy(to):
         return pltpu.make_async_remote_copy(
             src_ref=dense.at[to],
             dst_ref=z_in.at[sy],
-            send_sem=send_z.at[to],
-            recv_sem=recv_z.at[sy],
+            send_sem=share_sem.at[0],
+            recv_sem=share_sem.at[1],
             device_id=(sx, to),
             device_id_type=MESH,
         )
 
-    def corner_arrival(source):
-        return pltpu.make_async_remote_copy(
-            src_ref=dense.at[source],
-            dst_ref=z_in.at[source],
-            send_sem=send_z.at[source],
-            recv_sem=recv_z.at[source],
-            device_id=(sx, source),
-            device_id_type=MESH,
-        )
+    shares = pltpu.make_async_remote_copy(
+        src_ref=dense.at[pl.ds(0, ny - 1)],
+        dst_ref=z_in.at[pl.ds(0, ny - 1)],
+        send_sem=share_sem.at[0],
+        recv_sem=share_sem.at[1],
+        device_id=beside[0],
+        device_id_type=MESH,
+    )
 
     with jax.named_scope("corner_send"):
-        to_others(0, known, lambda to: corner_copy(to).start())
+        assemble(0, FIRST)
+        to_others(0, jnp.minimum(known, FIRST), lambda to: corner_copy(to).start())
+    if FIRST < ny:
+        with jax.named_scope("corner_rest"):
+            assemble(FIRST, ny)
 
     def selected(f, received):
         received = received.astype(F32)
@@ -256,11 +299,9 @@
     visc_rows = jnp.concatenate([jnp.full((HALF, width), visc[s], F32) for s in range(SUBS)], 0)
     size = SUBS * HALF
 
-    copies2 = []
     for c in range(2):
         with jax.named_scope(f"wait_traces{c}"):
-            for wait, _ in copies1[c]:
-                wait()
+            arrivals[1 + c]("wait_recv")
         with jax.named_scope(f"local{c}"):
             for f in range(4):
                 mine = own[c, f].reshape(size, width)
@@ -277,7 +318,6 @@
             def face(ref, f):
                 return ref[f * size : (f + 1) * size]
 
-            copies2.append([])
             for f in range(6):
                 others = [g for g in range(6) if g // 2 != f // 2]
                 value = face(w_s, f) + face(w_o, OPP[f])
@@ -286,18 +326,20 @@
                 )
                 local[c, f] = (visc_rows * value).astype(BF16)
                 if f < 4:
-                    copies2[c].append(exchange(local.at[c, f], in2.at[c], send2.at[c], recv2.at[c], f))
+                    exchange(*steps[3 + c], f)
             top, bottom = local[c, 4].astype(F32), local[c, 5].astype(F32)
             above = jnp.concatenate([bottom[HALF:], none], 0)
             below = jnp.concatenate([none, top[:-HALF]], 0)
             for f, value in ((4, top - above), (5, bottom - below)):
                 for s in range(SUBS):
                     applied[0, 0, s, f, c * HALF : (c + 1) * HALF] = value[s * HALF : (s + 1) * HALF]
+        if c == 0:
+            with jax.named_scope("corner_send_rest"):
+                to_others(FIRST, known, lambda to: corner_copy(to).start())
 
     def finish(c):
         with jax.named_scope(f"wait_local{c}"):
-            for wait, _ in copies2[c]:
-                wait()
+            arrivals[3 + c]("wait_recv")
         with jax.named_scope(f"applied{c}"):
             for f in range(4):
                 value = local[c, f].astype(F32) - selected(f, in2[c, f])
@@ -312,18 +354,29 @@
     finish(1)
 
     with jax.named_scope("corner_wait"):
-        to_others(0, ny, lambda source: corner_arrival(source).wait_recv())
+        shares.wait_recv()
     with jax.named_scope("corner_sum"):
         result = jnp.zeros((4, 128), F32)
         for source in range(ny):
             result += jnp.where(sy == source, dense[source], z_in[source])
-        coarse[:4] = result
-        coarse[4:] = pltpu.roll(result, 64, 1)
+        coarse[:4] = result[:, : RHS * COMPS]
+        coarse[4:] = pltpu.roll(result, 64, 1)[:, : RHS * COMPS]
 
     with jax.named_scope("sent"):
-        to_others(0, ny, lambda to: corner_copy(to).wait_send())
-        for _, wait in [*copies_y, *copies1[0], *copies1[1], *copies2[0], *copies2[1]]:
-            wait()
+        shares.wait_send()
+        for wait in arrivals:
+            wait("wait_send")
+
+
+def write_out(applied, coarse, applied_out, coarse_out, sems):
+    copies = (
+        pltpu.make_async_copy(applied, applied_out, sems.at[0]),
+        pltpu.make_async_copy(coarse, coarse_out, sems.at[1]),
+    )
+    for copy in copies:
+        copy.start()
+    for copy in copies:
+        copy.wait()
 
 
 def body(traces, viscosity, partner, corner_owner, self_block, opposite_block, cross_block, corner_map):
@@ -340,7 +393,7 @@
         functools.partial(kernel, nx, ny),
         out_shape=(
             jax.ShapeDtypeStruct(traces.shape, F32),
-            jax.ShapeDtypeStruct((8, 128), F32),
+            jax.ShapeDtypeStruct((8, RHS * COMPS), F32),
         ),
         in_specs=[pl.BlockSpec(memory_space=pltpu.HBM)] * 8,
         out_specs=(pl.BlockSpec(memory_space=vmem), pl.BlockSpec(memory_space=vmem)),
@@ -371,21 +424,23 @@
             vmem((ny, 4, 128), F32),
             vmem((ny, 4, 128), F32),
             dma((8,)),
-            dma((2, 4)),
-            dma((2, 4)),
-            dma((2, 4)),
-            dma((2, 4)),
-            dma((4,)),
-            dma((4,)),
-            dma((ny,)),
-            dma((ny,)),
+            dma((5,)),
+            dma((5,)),
+            dma((2,)),
             pltpu.SemaphoreType.REGULAR,
         ],
         compiler_params=pltpu.CompilerParams(
             collective_id=0, has_side_effects=True, vmem_limit_bytes=40 * 2**20
         ),
     )(*inputs)
-    return applied, coarse[:, : RHS * COMPS].T
+    applied, coarse = pl.pallas_call(
+        write_out,
+        out_shape=tuple(jax.ShapeDtypeStruct(value.shape, F32) for value in (applied, coarse)),
+        in_specs=[pl.BlockSpec(memory_space=pltpu.VMEM)] * 2,
+        out_specs=(pl.BlockSpec(memory_space=pltpu.HBM),) * 2,
+        scratch_shapes=[dma((2,))],
+    )(*(pltpu.with_memory_space_constraint(value, pltpu.VMEM) for value in (applied, coarse)))
+    return applied, coarse.T
 
 
 def solution(mesh):

time: 37.9 us -> 34.9 us (0.921)
  local copies, waits for them, and re-layouts: 1.61 us -> 0 us
  Pallas kernels: 35.5 us -> 33.9 us
    pallas_call x1, Pallas kernels: 35.5 us -> 32.9 us  [body(): pl.pallas_call(functools.partial(kernel, nx, ny), out_shape=(jax.ShapeDty...]
    pallas_call x0 -> x1, Pallas kernels: none -> 1.03 us  [body(): pl.pallas_call(write_out, out_shape=tuple((jax.ShapeDtypeStruct(value.sha...]
    unnamed x1 -> x0, local copies, waits for them, and re-layouts: 1.01 us -> none
    transpose x1 -> x0, local copies, waits for them, and re-layouts: 0.6 us -> none  [body(): return (applied, coarse[:, :RHS * COMPS].T)]
where the time goes in v5:
time: 34.9 us; the launch traced here: 34.5 us
  Pallas kernels  33.9 us (97%)
  between operations  0.64 us (2%)
    pallas_call x1, Pallas kernels, body(): pl.pallas_call(functools.partial(kernel, nx, ny), out_shape=(jax.ShapeDty...  32.9 us
    pallas_call x1, Pallas kernels, body(): pl.pallas_call(write_out, out_shape=tuple((jax.ShapeDtypeStruct(value.sha...  1.03 us

profile of v5, /device:TPU:1, one launch (start us, length us, event | category | flops | bytes accessed | tf_op | source)
XLA Modules:
  0.0 34.5 jit_solution(14447919156297515966)
XLA Ops:
  0.6 32.9 %shard_map.95 = (f32[1,1,4,6,16,768]{5,4,3,2,1,0:T(8,128)S(1)}, f32[8,48]{1,0:T(8,128)S(1)}) custom-call(bf16[1,1,4,6,16,768]{5,4,3,2,1,0:T(8,128)(2,1)} %traces.1, f32[1,1,4]{2,1,0:T(1,128)} %visc_in.1, s32[1,1,4,4]{3,2,1,0:T(4,128)} %partner_in.1, s32[1,1,4,8]{3,2,1,0:T(4,128)} %owner_in.1, bf16[768,768]{1,0:T(8,128)(2,1)} %self_in.1, ...), custom_call_target="tpu_custom_call" | custom-call | tf_op jit(solution)/shard_map/pallas_call | solution.py:392
  33.5 1.0 %shard_map.96 = (f32[1,1,4,6,16,768]{5,4,3,2,1,0:T(8,128)}, f32[8,48]{1,0:T(8,128)}) custom-call(f32[1,1,4,6,16,768]{5,4,3,2,1,0:T(8,128)S(1)} %get-tuple-element.6.applied, f32[8,48]{1,0:T(8,128)S(1)} %get-tuple-element.7.coarse), custom_call_target="tpu_custom_call" | custom-call | tf_op jit(solution)/shard_map/pallas_call | solution.py:436

commit v6 on v5

--- a/solution.py
+++ b/solution.py
@@ -194,9 +194,12 @@
                 for c in range(2):
                     out1[c, f] = own[c, f].reshape(SUBS * HALF, width).astype(BF16)
 
-    for c in range(2):
-        for f in range(4):
-            exchange(*steps[1 + c], f)
+    def send_traces():
+        for c in range(2):
+            for f in range(4):
+                exchange(*steps[1 + c], f)
+
+    pl.when(z < ny // QUAD // 2)(send_traces)
     to_others(0, z * QUAD, lambda to: signal(far_sem, (sx, to)))
 
     for f in range(4):
@@ -280,9 +283,11 @@
     with jax.named_scope("corner_send"):
         assemble(0, FIRST)
         to_others(0, jnp.minimum(known, FIRST), lambda to: corner_copy(to).start())
+    pl.when(z >= ny // QUAD // 2)(send_traces)
     if FIRST < ny:
         with jax.named_scope("corner_rest"):
             assemble(FIRST, ny)
+            to_others(FIRST, known, lambda to: corner_copy(to).start())
 
     def selected(f, received):
         received = received.astype(F32)
@@ -333,9 +338,6 @@
             for f, value in ((4, top - above), (5, bottom - below)):
                 for s in range(SUBS):
                     applied[0, 0, s, f, c * HALF : (c + 1) * HALF] = value[s * HALF : (s + 1) * HALF]
-        if c == 0:
-            with jax.named_scope("corner_send_rest"):
-                to_others(FIRST, known, lambda to: corner_copy(to).start())
 
     def finish(c):
         with jax.named_scope(f"wait_local{c}"):
@@ -369,10 +371,9 @@
 
 
 def write_out(applied, coarse, applied_out, coarse_out, sems):
-    copies = (
-        pltpu.make_async_copy(applied, applied_out, sems.at[0]),
-        pltpu.make_async_copy(coarse, coarse_out, sems.at[1]),
-    )
+    copies = [pltpu.make_async_copy(coarse, coarse_out, sems.at[SUBS])]
+    for s in range(SUBS):
+        copies.append(pltpu.make_async_copy(applied.at[0, 0, s], applied_out.at[0, 0, s], sems.at[s]))
     for copy in copies:
         copy.start()
     for copy in copies:
@@ -438,7 +439,7 @@
         out_shape=tuple(jax.ShapeDtypeStruct(value.shape, F32) for value in (applied, coarse)),
         in_specs=[pl.BlockSpec(memory_space=pltpu.VMEM)] * 2,
         out_specs=(pl.BlockSpec(memory_space=pltpu.HBM),) * 2,
-        scratch_shapes=[dma((2,))],
+        scratch_shapes=[dma((SUBS + 1,))],
     )(*(pltpu.with_memory_space_constraint(value, pltpu.VMEM) for value in (applied, coarse)))
     return applied, coarse.T
 

time: 34.9 us -> 33.9 us (0.971)
  Pallas kernels: 33.9 us -> 33.1 us
    pallas_call x1, Pallas kernels: 32.9 us -> 32.1 us  [body(): pl.pallas_call(functools.partial(kernel, nx, ny), out_shape=(jax.ShapeDty...]
where the time goes in v6:
time: 33.9 us; the launch traced here: 33.7 us
  Pallas kernels  33.1 us (98%)
  between operations  0.64 us (2%)
    pallas_call x1, Pallas kernels, body(): pl.pallas_call(functools.partial(kernel, nx, ny), out_shape=(jax.ShapeDty...  32.1 us
    pallas_call x1, Pallas kernels, body(): pl.pallas_call(write_out, out_shape=tuple((jax.ShapeDtypeStruct(value.sha...  1.05 us

profile of v6, /device:TPU:1, one launch (start us, length us, event | category | flops | bytes accessed | tf_op | source)
XLA Modules:
  0.0 33.7 jit_solution(7596674539420563997)
XLA Ops:
  0.6 32.1 %shard_map.95 = (f32[1,1,4,6,16,768]{5,4,3,2,1,0:T(8,128)S(1)}, f32[8,48]{1,0:T(8,128)S(1)}) custom-call(bf16[1,1,4,6,16,768]{5,4,3,2,1,0:T(8,128)(2,1)} %traces.1, f32[1,1,4]{2,1,0:T(1,128)} %visc_in.1, s32[1,1,4,4]{3,2,1,0:T(4,128)} %partner_in.1, s32[1,1,4,8]{3,2,1,0:T(4,128)} %owner_in.1, bf16[768,768]{1,0:T(8,128)(2,1)} %self_in.1, ...), custom_call_target="tpu_custom_call" | custom-call | tf_op jit(solution)/shard_map/pallas_call | solution.py:393
  32.7 1.1 %shard_map.96 = (f32[1,1,4,6,16,768]{5,4,3,2,1,0:T(8,128)}, f32[8,48]{1,0:T(8,128)}) custom-call(f32[1,1,4,6,16,768]{5,4,3,2,1,0:T(8,128)S(1)} %get-tuple-element.6.applied, f32[8,48]{1,0:T(8,128)S(1)} %get-tuple-element.7.coarse), custom_call_target="tpu_custom_call" | custom-call | tf_op jit(solution)/shard_map/pallas_call | solution.py:437

commit v7 on v6

--- a/solution.py
+++ b/solution.py
@@ -18,7 +18,7 @@
 BLOCK = 32
 QUAD = 4
 OPP = (1, 0, 3, 2, 5, 4)
-FIRST = 4 * QUAD
+FIRST = 3 * QUAD
 
 
 def nt_dot(left, right):
@@ -145,31 +145,39 @@
         faces = [jnp.concatenate([cmap[f].astype(F32), pad], 0) for f in range(6)]
         straight = jnp.concatenate(faces, 0).astype(BF16)
 
-    def through(name, matrix):
-        loads[name].wait()
-        product = nt_dot(straight, matrix[...])
-        return [product[f * BLOCK : (f + 1) * BLOCK] for f in range(6)]
-
+    def through(rows, matrix):
+        product = nt_dot(rows, matrix[...])
+        return [product[at : at + BLOCK] for at in range(0, rows.shape[0], BLOCK)]
+
+    half = 4 * BLOCK
     with jax.named_scope("weights_cross"):
-        cross = through("cross", c_mat)
+        loads["cross"].wait()
+        cross = through(straight, c_mat)
     with jax.named_scope("weights_self"):
-        same = through("self", s_mat)
+        loads["self"].wait()
+        same = through(straight[:half], s_mat)
     with jax.named_scope("weights_opposite"):
-        across = through("opp", o_mat)
+        loads["opp"].wait()
+        across = through(straight[:half], o_mat)
         pairs = [cross[0] + cross[1], cross[2] + cross[3], cross[4] + cross[5]]
         adjacent = [pairs[1] + pairs[2], pairs[0] + pairs[2], pairs[0] + pairs[1]]
-        weight = [same[f] + across[OPP[f]] + adjacent[f // 2] for f in range(6)]
+        weight = [same[f] + across[OPP[f]] + adjacent[f // 2] for f in range(4)]
+        w_hi[:half], w_lo[:half] = split(jnp.concatenate(weight, 0), 2)
+
+    def z_weights():
+        same, across = through(straight[half:], s_mat), through(straight[half:], o_mat)
+        weight = [same[f] + across[1 - f] + adjacent[2] for f in range(2)]
         weight.append(jnp.zeros((2 * BLOCK, width), F32))
-        w_hi[...], w_lo[...] = split(jnp.concatenate(weight, 0), 2)
+        w_hi[half:], w_lo[half:] = split(jnp.concatenate(weight, 0), 2)
 
     def value_of(s, f, face, to):
-        tile = y_all[s, f, :, face // 4 * 128 : face // 4 * 128 + 128]
-        return jnp.where(block == to, moved(tile, to - face % 4), 0.0)
+        return jnp.where(block == to, moved(y_all[s, f], to - face % 4), 0.0)
 
     def values(f):
         flat = raw[:, f : f + 2].reshape(SUBS * 2 * RHS, width)
-        both = nt_dot(flat, w_hi[...]) + nt_dot(flat, w_lo[...])
-        y_all[:, f : f + 2] = both.reshape(SUBS, 2, RHS, 8 * BLOCK)
+        rows = pl.ds(f // 4 * half, half)
+        both = nt_dot(flat, w_hi[rows]) + nt_dot(flat, w_lo[rows])
+        y_all[:, f : f + 2] = both.reshape(SUBS, 2, RHS, half)
 
     for f in (0, 2):
         with jax.named_scope(f"values{f}"):
@@ -224,6 +232,7 @@
                 owners = jnp.where((lane >= first) & (lane < first + COMPS), owner[s, m], owners)
         unknown = lax.broadcasted_iota(jnp.int32, (8 * ny, 1), 0)
         onehot = jnp.where(unknown == owners, 1.0, 0.0).astype(BF16)
+        z_weights()
         values(4)
         parts = jnp.zeros((RHS, 128), F32)
         for s in range(SUBS):
@@ -250,7 +259,7 @@
         comp = lax.rem(lax.rem(lane, BLOCK), COMPS)
         for c in range(COMPS):
             stacked[pl.ds(c, RHS, stride=COMPS)] = jnp.where(comp == c, parts, 0.0)
-        pieces = split(stacked[...], 3)
+        pieces = split(stacked[...], 2)
 
     def assemble(first, last):
         total = sum(nt_dot(onehot[first * 8 : last * 8], piece) for piece in pieces)
@@ -418,7 +427,7 @@
             vmem((2, 4, size, width), BF16),
             vmem((8 * BLOCK, width), BF16),
             vmem((8 * BLOCK, width), BF16),
-            vmem((SUBS, 6, RHS, 8 * BLOCK), F32),
+            vmem((SUBS, 6, RHS, 4 * BLOCK), F32),
             vmem((4, RHS, 128), F32),
             vmem((4, RHS, 128), F32),
             vmem((RHS * COMPS, 128), F32),

time: 33.9 us -> 33.5 us (0.988)
  Pallas kernels: 33.1 us -> 32.7 us
    pallas_call x1, Pallas kernels: 32.1 us -> 31.7 us  [body(): pl.pallas_call(functools.partial(kernel, nx, ny), out_shape=(jax.ShapeDty...]
where the time goes in v7:
time: 33.5 us; the launch traced here: 33.4 us
  Pallas kernels  32.7 us (98%)
  between operations  0.64 us (2%)
    pallas_call x1, Pallas kernels, body(): pl.pallas_call(functools.partial(kernel, nx, ny), out_shape=(jax.ShapeDty...  31.7 us
    pallas_call x1, Pallas kernels, body(): pl.pallas_call(write_out, out_shape=tuple((jax.ShapeDtypeStruct(value.sha...  1.05 us

profile of v7, /device:TPU:1, one launch (start us, length us, event | category | flops | bytes accessed | tf_op | source)
XLA Modules:
  0.0 33.4 jit_solution(5878603171898285861)
XLA Ops:
  0.6 31.7 %shard_map.95 = (f32[1,1,4,6,16,768]{5,4,3,2,1,0:T(8,128)S(1)}, f32[8,48]{1,0:T(8,128)S(1)}) custom-call(bf16[1,1,4,6,16,768]{5,4,3,2,1,0:T(8,128)(2,1)} %traces.1, f32[1,1,4]{2,1,0:T(1,128)} %visc_in.1, s32[1,1,4,4]{3,2,1,0:T(4,128)} %partner_in.1, s32[1,1,4,8]{3,2,1,0:T(4,128)} %owner_in.1, bf16[768,768]{1,0:T(8,128)(2,1)} %self_in.1, ...), custom_call_target="tpu_custom_call" | custom-call | tf_op jit(solution)/shard_map/pallas_call | solution.py:402
  32.3 1.1 %shard_map.96 = (f32[1,1,4,6,16,768]{5,4,3,2,1,0:T(8,128)}, f32[8,48]{1,0:T(8,128)}) custom-call(f32[1,1,4,6,16,768]{5,4,3,2,1,0:T(8,128)S(1)} %get-tuple-element.6.applied, f32[8,48]{1,0:T(8,128)S(1)} %get-tuple-element.7.coarse), custom_call_target="tpu_custom_call" | custom-call | tf_op jit(solution)/shard_map/pallas_call | solution.py:446
